TPU v7x, 32 devices: a whole 2x2x4 slice. The times are simulated.
32 devices in a mesh: ctx: 2 (over y), head: 4 (over x, core), dp: 4 (over z).
Axes of the slice: x: 2, y: 2, z: 4, core: 2. Of those that a mesh axis runs over, the one named last changes fastest.
Arguments:
- query_states: bfloat16 [4096, 8192], P(('dp', 'ctx'), 'head'), parts along dimension 0, may hold values from -6 to 6
- key_states: bfloat16 [4096, 1024], P(('dp', 'ctx'), 'head'), parts along dimension 0, may hold values from -6 to 6
- value_state_rows: bfloat16 [4096, 1024], P(('dp', 'ctx'), 'head'), parts along dimension 0, may hold values from -6 to 6
- grad_out: bfloat16 [4096, 8192], P(('dp', 'ctx'), 'head'), parts along dimension 0, may hold values from -6 to 6
- vis_blocks: int32 [32, 6], P('dp'), parts along dimension 0, may hold values from 0 to 7, as said below
- vis_count: int32 [32], P('dp'), parts along dimension 0, may hold values from 1 to 6
- vis_len: int32 [32, 6], P('dp'), parts along dimension 0, may hold values from 1 to 128, as said below
Outputs:
- attention: bfloat16 [4096, 8192], P(('dp', 'ctx'), 'head'), parts along dimension 0
- grad_query: bfloat16 [4096, 8192], P(('dp', 'ctx'), 'head'), parts along dimension 0
- grad_key: bfloat16 [4096, 1024], P(('dp', 'ctx'), 'head'), parts along dimension 0
- grad_value: bfloat16 [4096, 1024], P(('dp', 'ctx'), 'head'), parts along dimension 0
There are 4 independent parts, one for each index of `dp`. A program takes and returns all parts, laid end to end along the dimension named above; each array names one. Nothing has to cross between parts.
Inputs may be any that keep to these rules, and one draw needn't show every extreme that they name: `vis_blocks`: slot 0 of row b is b itself; live slots 1 to vis_count[b] - 1 hold distinct blocks before b; slots at or past vis_count[b] hold b. Over the live slots of the 4 rows of one group of 4 consecutive query blocks, at most 2 distinct blocks of any other such group appear. `vis_len`: slot 0 and slots at or past vis_count hold 128.
All inputs are finite; a program needn't handle non-finite values.
Results may differ from a plain program's by a relative error of at most 0.012.
Values may be sent and summed in bfloat16 or wider, within the bound.
No kernel may reach another device: no remote copies, remote signals or barrier semaphores. Data moves between devices by JAX's collectives and lax.ppermute only.
A program may use at most 128 MiB of HBM per device.

v0:
```python
import math

import jax
import jax.numpy as jnp
from jax import lax
from jax.sharding import PartitionSpec as P

HEAD_SIZE = 128
MASK_BLOCK_SIZE = 128


masked_score = -1e30


def attend(
    query_block_rows,
    gradient_block_rows,
    key_value_slots,
    block_id,
    row_blocks,
    row_count,
    row_lens,
):
    block_rows = query_block_rows.shape[0]
    total_slot_count = key_value_slots.shape[0]
    key_value_width = key_value_slots.shape[2] // 2
    kv_heads = key_value_width // HEAD_SIZE
    group_width_count = query_block_rows.shape[1] // key_value_width
    inv_root = 1.0 / math.sqrt(HEAD_SIZE)
    query_rows = query_block_rows.reshape(block_rows, kv_heads, group_width_count, HEAD_SIZE)
    output_gradients = gradient_block_rows.reshape(
        block_rows, kv_heads, group_width_count, HEAD_SIZE
    )
    key_portion = key_value_slots[:, :, :key_value_width].reshape(
        total_slot_count, block_rows, kv_heads, HEAD_SIZE
    )
    value_portion = key_value_slots[:, :, key_value_width:].reshape(
        total_slot_count, block_rows, kv_heads, HEAD_SIZE
    )
    query_pos = jnp.arange(block_rows, dtype=jnp.int32)[:, None, None]
    key_pos = jnp.arange(block_rows, dtype=jnp.int32)[None, None, :]
    slot_pos = jnp.arange(total_slot_count, dtype=jnp.int32)[None, :, None]
    visible = (slot_pos < row_count) & (key_pos < row_lens[None, :, None])
    visible = visible & ((row_blocks[None, :, None] != block_id) | (key_pos <= query_pos))
    scores = (
        jnp.einsum("qgrd,vkgd->grqvk", query_rows, key_portion, preferred_element_type=jnp.float32)
        * inv_root
    )
    row_max = jnp.max(jnp.where(visible, scores, masked_score), axis=(3, 4), keepdims=True)
    weights = jnp.exp(jnp.where(visible, scores - row_max, masked_score))
    soft_probs = weights / jnp.sum(weights, axis=(3, 4), keepdims=True)
    probs_low = soft_probs.astype(jnp.bfloat16)
    attention = jnp.einsum(
        "grqvk,vkgd->qgrd", probs_low, value_portion, preferred_element_type=jnp.float32
    )
    attention = attention.astype(jnp.bfloat16).reshape(block_rows, -1)
    dprobs = jnp.einsum(
        "qgrd,vkgd->grqvk", output_gradients, value_portion, preferred_element_type=jnp.float32
    )
    row_delta = jnp.sum(soft_probs * dprobs, axis=(3, 4), keepdims=True)
    dscores = (soft_probs * (dprobs - row_delta) * inv_root).astype(jnp.bfloat16)
    grad_query = jnp.einsum(
        "grqvk,vkgd->qgrd", dscores, key_portion, preferred_element_type=jnp.float32
    )
    grad_query = grad_query.astype(jnp.bfloat16).reshape(block_rows, -1)
    grad_keys = jnp.einsum(
        "grqvk,qgrd->vkgd", dscores, query_rows, preferred_element_type=jnp.float32
    )
    grad_values = jnp.einsum(
        "grqvk,qgrd->vkgd", probs_low, output_gradients, preferred_element_type=jnp.float32
    )
    grad_keys = grad_keys.reshape(total_slot_count, block_rows, key_value_width)
    grad_values = grad_values.reshape(total_slot_count, block_rows, key_value_width)
    return (attention, grad_query, jnp.concatenate([grad_keys, grad_values], axis=2))


def body(query_states, key_states, value_state_rows, grad_out, vis_blocks, vis_count, vis_len):
    shard_tokens = query_states.shape[0]
    per_shard = shard_tokens // MASK_BLOCK_SIZE
    total_blocks = vis_blocks.shape[0]
    total_slot_count = vis_blocks.shape[1]
    my_index = lax.axis_index("ctx")
    local_kv = jnp.concatenate([key_states, value_state_rows], axis=1)
    kv_total = local_kv.shape[1]
    key_value_width = key_states.shape[1]
    first_block = my_index * per_shard
    my_blocks = lax.dynamic_slice_in_dim(vis_blocks, first_block, per_shard, 0)
    my_count = lax.dynamic_slice_in_dim(vis_count, first_block, per_shard, 0)
    my_lens = lax.dynamic_slice_in_dim(vis_len, first_block, per_shard, 0)
    block_ids = first_block + jnp.arange(per_shard, dtype=jnp.int32)
    gathered = lax.all_gather(local_kv, "ctx", axis=0, tiled=True)
    all_blocks = gathered.reshape(total_blocks, MASK_BLOCK_SIZE, kv_total)
    key_value_slots = all_blocks[my_blocks]

    def one_block(pieces):
        (
            query_block_rows,
            gradient_block_rows,
            slot_block,
            block_id,
            row_blocks,
            row_count,
            row_lens,
        ) = pieces
        return attend(
            query_block_rows,
            gradient_block_rows,
            slot_block,
            block_id,
            row_blocks,
            row_count,
            row_lens,
        )

    attention, grad_query, slot_grads = lax.map(
        one_block,
        (
            query_states.reshape(per_shard, MASK_BLOCK_SIZE, -1),
            grad_out.reshape(per_shard, MASK_BLOCK_SIZE, -1),
            key_value_slots,
            block_ids,
            my_blocks,
            my_count,
            my_lens,
        ),
    )
    flat_grads = slot_grads.reshape(per_shard * total_slot_count, MASK_BLOCK_SIZE * kv_total)
    all_index = jnp.arange(total_blocks, dtype=jnp.int32)
    one_hot = (all_index[:, None] == my_blocks.reshape(-1)[None, :]).astype(jnp.float32)
    dense_part = jnp.dot(
        one_hot, flat_grads, precision=lax.Precision.HIGHEST, preferred_element_type=jnp.float32
    )
    summed = lax.psum_scatter(
        dense_part.reshape(total_blocks * MASK_BLOCK_SIZE, kv_total).astype(jnp.bfloat16),
        "ctx",
        scatter_dimension=0,
        tiled=True,
    ).astype(jnp.float32)
    grad_key = summed[:, :key_value_width].astype(jnp.bfloat16)
    grad_value = summed[:, key_value_width:].astype(jnp.bfloat16)
    return (
        attention.reshape(shard_tokens, -1),
        grad_query.reshape(shard_tokens, -1),
        grad_key,
        grad_value,
    )


def solution(mesh):
    in_specs = (
        P(("dp", "ctx"), "head"),
        P(("dp", "ctx"), "head"),
        P(("dp", "ctx"), "head"),
        P(("dp", "ctx"), "head"),
        P("dp", None),
        P("dp"),
        P("dp", None),
    )
    out_specs = (
        P(("dp", "ctx"), "head"),
        P(("dp", "ctx"), "head"),
        P(("dp", "ctx"), "head"),
        P(("dp", "ctx"), "head"),
    )
    return jax.shard_map(body, mesh=mesh, in_specs=in_specs, out_specs=out_specs, check_vma=False)
```

profile of v0, /device:TPU:0, one launch (start us, length us, event | category | flops | bytes accessed | tf_op | source)
XLA Modules:
  0.0 249.9 jit_solution(3337640436929024716)
XLA Ops:
  7.2 1.9 pad_maximum_fusion
  11.9 21.7 %all-gather.2.cloned.1.call-done = bf16[1024,512]{1,0:T(8,128)(2,1)} async-done(((bf16[512,512]{1,0:T(8,128)(2,1)}), bf16[1024,512]{1,0:T(8,128)(2,1)}) %all-gather.2.cloned.1.call-update) | async-done | bytes 1048592 | tf_op jit(solution)/shard_map/all_gather | solution.py:91
  33.6 3.7 %gather_fusion = bf16[24,128,512]{2,1,0:T(8,128)(2,1)} fusion(bf16[8,128,512]{2,1,0:T(8,128)(2,1)} %bitcast.184, s32[1024]{0:T(1024)S(1)} %pad_clamp_fusion), kind=kCustom, calls=%fused_computation | custom fusion | bytes 6291552 | tf_op jit(solution)/shard_map/gather | solution.py:93
  37.3 173.3 %while.14 = (s32[]{:T(128)}, bf16[4,128,2048]{2,1,0:T(8,128)(2,1)}, bf16[4,128,2048]{2,1,0:T(8,128)(2,1)}, f32[4,6,128,512]{3,2,1,0:T(8,128)}, bf16[4,6,128,512]...) while((s32[]{:T(128)}, bf16[4,128,2048]{2,1,0:T(8,128)(2,1)}, ...), condition=%wide.region_4.5_spmd, body=%wide.region_0.4_spmd.sunk | while | flops 2451648000 | bytes 174140432 | solution.py:115
  38.6 1.2 dynamic_slice.62
  45.7 2.6 %copy-done.1 = f32[2,6,128,128,8]{3,2,4,1,0:T(8,128)} copy-done((f32[2,6,128,128,8]{3,2,4,1,0:T(8,128)}, f32[2,6,128,128,8]{3,2,4,1,0:T(8,128)S(1)}, u32[]{:S(2)}) %copy-start.1) | copy-done | bytes 6291480 | tf_op jit(solution)/shard_map/while
  48.4 1.3 fusion.77
  49.7 1.9 constant_dynamic-slice_fusion.13
  51.6 1.5 copy.139
  53.1 4.4 %fusion.78 = (f32[2,8,128]{2,1,0:T(8,128)S(1)}, f32[2,6,128,128,8]{3,2,4,1,0:T(8,128)S(1)}) fusion(f32[2,8,128]{2,1,0:T(8,128)S(1)} %fusion.77, f32[2,8,128]{2,1,0:T(8,128)S(1)} %get-tuple-element.192, f32[2,6,128,128,8]{3,2,4,1,0:T(8,128)} %copy-done.1, pred[128,6,128]{0,2,1:T(8,128)(4,1)S(1)} %or_and_fusion.2, ...), kind=kOutput, calls=%fused_computation.3.clone.1 | convolution fusion | flops 412088320 | bytes 13623296 | tf_op jit(solution)/shard_map/while/body/eval_jaxpr/qgrd,vkgd->grqvk/dot_general | solution.py:57
  57.6 2.6 %fusion.79 = (bf16[2,8,128,6,128]{2,4,1,3,0:T(8,128)(2,1)S(1)}, bf16[2,8,128,6,128]{2,4,1,3,0:T(8,128)(2,1)S(1)}) fusion(f32[2,6,128,128,8]{3,2,4,1,0:T(8,128)S(1)} %get-tuple-element.194, f32[2,8,128]{2,1,0:T(8,128)S(1)} %get-tuple-element.195, f32[2,8,128]{2,1,0:T(8,128)S(1)} %fusion.77, f32[2,8,128]{2,1,0:T(8,128)S(1)} %get-tuple-element.192, ...), kind=kLoop, calls=%fused_computation.6.clone.1 | loop fusion | flops 14155776 | bytes 18997248 | tf_op jit(solution)/shard_map/while/body/eval_jaxpr/convert_element_type | solution.py:61
  63.1 1.3 maximum_bitcast_fusion.2
  64.4 3.2 %copy.144 = f32[1,6,128,512]{3,2,1,0:T(8,128)} copy(f32[1,6,128,512]{2,3,1,0:T(8,128)} %maximum_bitcast_fusion.2) | data formatting | bytes 3145728 | tf_op jit(solution)/shard_map/while/body/jit(dynamic_update_index_in_dim)/dynamic_update_slice | solution.py:115
  67.5 2.8 %constant_dynamic-update-slice_fusion.6 = f32[4,6,128,512]{3,2,1,0:T(8,128)} fusion(f32[4,6,128,512]{3,2,1,0:T(8,128)} %get-tuple-element.215, f32[1,6,128,512]{3,2,1,0:T(8,128)} %copy.144, s32[]{:T(128)} %get-tuple-element.212), kind=kLoop, calls=%fused_computation.35.clone.1 | loop fusion | bytes 3146240 | tf_op jit(solution)/shard_map/while/body/jit(dynamic_update_index_in_dim)/dynamic_update_slice | solution.py:115
  70.3 3.5 %fusion.81 = bf16[2,128,8,128]{3,1,2,0:T(8,128)(2,1)} fusion(bf16[2,8,128,6,128]{2,4,1,3,0:T(8,128)(2,1)} %copy-done.4, bf16[6,128,2,128,1]{1,3,2,0,4:T(8,128)(2,1)} %bitcast.183), kind=kOutput, calls=%fused_computation.24.clone.1 | convolution fusion | flops 402915328 | bytes 4063232 | tf_op jit(solution)/shard_map/while/body/eval_jaxpr/grqvk,vkgd->qgrd/dot_general | solution.py:53
  73.8 2.0 copy.141
  75.8 1.4 fusion.80
  78.5 2.2 constant_dynamic-update-slice_fusion.5
  82.0 1.2 dynamic_slice.62
  89.1 2.6 %copy-done.1 = f32[2,6,128,128,8]{3,2,4,1,0:T(8,128)} copy-done((f32[2,6,128,128,8]{3,2,4,1,0:T(8,128)}, f32[2,6,128,128,8]{3,2,4,1,0:T(8,128)S(1)}, u32[]{:S(2)}) %copy-start.1) | copy-done | bytes 6291480 | tf_op jit(solution)/shard_map/while
  91.7 1.3 fusion.77
  93.0 1.9 constant_dynamic-slice_fusion.13
  94.9 1.5 copy.139
  96.4 4.4 %fusion.78 = (f32[2,8,128]{2,1,0:T(8,128)S(1)}, f32[2,6,128,128,8]{3,2,4,1,0:T(8,128)S(1)}) fusion(f32[2,8,128]{2,1,0:T(8,128)S(1)} %fusion.77, f32[2,8,128]{2,1,0:T(8,128)S(1)} %get-tuple-element.192, f32[2,6,128,128,8]{3,2,4,1,0:T(8,128)} %copy-done.1, pred[128,6,128]{0,2,1:T(8,128)(4,1)S(1)} %or_and_fusion.2, ...), kind=kOutput, calls=%fused_computation.3.clone.1 | convolution fusion | flops 412088320 | bytes 13623296 | tf_op jit(solution)/shard_map/while/body/eval_jaxpr/qgrd,vkgd->grqvk/dot_general | solution.py:57
  100.9 2.6 %fusion.79 = (bf16[2,8,128,6,128]{2,4,1,3,0:T(8,128)(2,1)S(1)}, bf16[2,8,128,6,128]{2,4,1,3,0:T(8,128)(2,1)S(1)}) fusion(f32[2,6,128,128,8]{3,2,4,1,0:T(8,128)S(1)} %get-tuple-element.194, f32[2,8,128]{2,1,0:T(8,128)S(1)} %get-tuple-element.195, f32[2,8,128]{2,1,0:T(8,128)S(1)} %fusion.77, f32[2,8,128]{2,1,0:T(8,128)S(1)} %get-tuple-element.192, ...), kind=kLoop, calls=%fused_computation.6.clone.1 | loop fusion | flops 14155776 | bytes 18997248 | tf_op jit(solution)/shard_map/while/body/eval_jaxpr/convert_element_type | solution.py:61
  106.4 1.3 maximum_bitcast_fusion.2
  107.7 3.2 %copy.144 = f32[1,6,128,512]{3,2,1,0:T(8,128)} copy(f32[1,6,128,512]{2,3,1,0:T(8,128)} %maximum_bitcast_fusion.2) | data formatting | bytes 3145728 | tf_op jit(solution)/shard_map/while/body/jit(dynamic_update_index_in_dim)/dynamic_update_slice | solution.py:115
  110.9 2.8 %constant_dynamic-update-slice_fusion.6 = f32[4,6,128,512]{3,2,1,0:T(8,128)} fusion(f32[4,6,128,512]{3,2,1,0:T(8,128)} %get-tuple-element.215, f32[1,6,128,512]{3,2,1,0:T(8,128)} %copy.144, s32[]{:T(128)} %get-tuple-element.212), kind=kLoop, calls=%fused_computation.35.clone.1 | loop fusion | bytes 3146240 | tf_op jit(solution)/shard_map/while/body/jit(dynamic_update_index_in_dim)/dynamic_update_slice | solution.py:115
  113.6 3.5 %fusion.81 = bf16[2,128,8,128]{3,1,2,0:T(8,128)(2,1)} fusion(bf16[2,8,128,6,128]{2,4,1,3,0:T(8,128)(2,1)} %copy-done.4, bf16[6,128,2,128,1]{1,3,2,0,4:T(8,128)(2,1)} %bitcast.183), kind=kOutput, calls=%fused_computation.24.clone.1 | convolution fusion | flops 402915328 | bytes 4063232 | tf_op jit(solution)/shard_map/while/body/eval_jaxpr/grqvk,vkgd->qgrd/dot_general | solution.py:53
  117.1 2.0 copy.141
  119.1 1.4 fusion.80
  121.8 2.2 constant_dynamic-update-slice_fusion.5
  125.3 1.2 dynamic_slice.62
  132.4 2.6 %copy-done.1 = f32[2,6,128,128,8]{3,2,4,1,0:T(8,128)} copy-done((f32[2,6,128,128,8]{3,2,4,1,0:T(8,128)}, f32[2,6,128,128,8]{3,2,4,1,0:T(8,128)S(1)}, u32[]{:S(2)}) %copy-start.1) | copy-done | bytes 6291480 | tf_op jit(solution)/shard_map/while
  135.0 1.3 fusion.77
  136.3 1.9 constant_dynamic-slice_fusion.13
  138.3 1.5 copy.139
  139.7 4.4 %fusion.78 = (f32[2,8,128]{2,1,0:T(8,128)S(1)}, f32[2,6,128,128,8]{3,2,4,1,0:T(8,128)S(1)}) fusion(f32[2,8,128]{2,1,0:T(8,128)S(1)} %fusion.77, f32[2,8,128]{2,1,0:T(8,128)S(1)} %get-tuple-element.192, f32[2,6,128,128,8]{3,2,4,1,0:T(8,128)} %copy-done.1, pred[128,6,128]{0,2,1:T(8,128)(4,1)S(1)} %or_and_fusion.2, ...), kind=kOutput, calls=%fused_computation.3.clone.1 | convolution fusion | flops 412088320 | bytes 13623296 | tf_op jit(solution)/shard_map/while/body/eval_jaxpr/qgrd,vkgd->grqvk/dot_general | solution.py:57
  144.2 2.6 %fusion.79 = (bf16[2,8,128,6,128]{2,4,1,3,0:T(8,128)(2,1)S(1)}, bf16[2,8,128,6,128]{2,4,1,3,0:T(8,128)(2,1)S(1)}) fusion(f32[2,6,128,128,8]{3,2,4,1,0:T(8,128)S(1)} %get-tuple-element.194, f32[2,8,128]{2,1,0:T(8,128)S(1)} %get-tuple-element.195, f32[2,8,128]{2,1,0:T(8,128)S(1)} %fusion.77, f32[2,8,128]{2,1,0:T(8,128)S(1)} %get-tuple-element.192, ...), kind=kLoop, calls=%fused_computation.6.clone.1 | loop fusion | flops 14155776 | bytes 18997248 | tf_op jit(solution)/shard_map/while/body/eval_jaxpr/convert_element_type | solution.py:61
  149.7 1.3 maximum_bitcast_fusion.2
  151.0 3.2 %copy.144 = f32[1,6,128,512]{3,2,1,0:T(8,128)} copy(f32[1,6,128,512]{2,3,1,0:T(8,128)} %maximum_bitcast_fusion.2) | data formatting | bytes 3145728 | tf_op jit(solution)/shard_map/while/body/jit(dynamic_update_index_in_dim)/dynamic_update_slice | solution.py:115
  154.2 2.8 %constant_dynamic-update-slice_fusion.6 = f32[4,6,128,512]{3,2,1,0:T(8,128)} fusion(f32[4,6,128,512]{3,2,1,0:T(8,128)} %get-tuple-element.215, f32[1,6,128,512]{3,2,1,0:T(8,128)} %copy.144, s32[]{:T(128)} %get-tuple-element.212), kind=kLoop, calls=%fused_computation.35.clone.1 | loop fusion | bytes 3146240 | tf_op jit(solution)/shard_map/while/body/jit(dynamic_update_index_in_dim)/dynamic_update_slice | solution.py:115
  156.9 3.5 %fusion.81 = bf16[2,128,8,128]{3,1,2,0:T(8,128)(2,1)} fusion(bf16[2,8,128,6,128]{2,4,1,3,0:T(8,128)(2,1)} %copy-done.4, bf16[6,128,2,128,1]{1,3,2,0,4:T(8,128)(2,1)} %bitcast.183), kind=kOutput, calls=%fused_computation.24.clone.1 | convolution fusion | flops 402915328 | bytes 4063232 | tf_op jit(solution)/shard_map/while/body/eval_jaxpr/grqvk,vkgd->qgrd/dot_general | solution.py:53
  160.4 2.0 copy.141
  162.4 1.4 fusion.80
  165.1 2.2 constant_dynamic-update-slice_fusion.5
  175.7 2.6 %copy-done.1 = f32[2,6,128,128,8]{3,2,4,1,0:T(8,128)} copy-done((f32[2,6,128,128,8]{3,2,4,1,0:T(8,128)}, f32[2,6,128,128,8]{3,2,4,1,0:T(8,128)S(1)}, u32[]{:S(2)}) %copy-start.1) | copy-done | bytes 6291480 | tf_op jit(solution)/shard_map/while
  178.4 1.3 fusion.77
  179.6 1.9 constant_dynamic-slice_fusion.13
  181.6 1.5 copy.139
  183.1 4.4 %fusion.78 = (f32[2,8,128]{2,1,0:T(8,128)S(1)}, f32[2,6,128,128,8]{3,2,4,1,0:T(8,128)S(1)}) fusion(f32[2,8,128]{2,1,0:T(8,128)S(1)} %fusion.77, f32[2,8,128]{2,1,0:T(8,128)S(1)} %get-tuple-element.192, f32[2,6,128,128,8]{3,2,4,1,0:T(8,128)} %copy-done.1, pred[128,6,128]{0,2,1:T(8,128)(4,1)S(1)} %or_and_fusion.2, ...), kind=kOutput, calls=%fused_computation.3.clone.1 | convolution fusion | flops 412088320 | bytes 13623296 | tf_op jit(solution)/shard_map/while/body/eval_jaxpr/qgrd,vkgd->grqvk/dot_general | solution.py:57
  187.5 2.6 %fusion.79 = (bf16[2,8,128,6,128]{2,4,1,3,0:T(8,128)(2,1)S(1)}, bf16[2,8,128,6,128]{2,4,1,3,0:T(8,128)(2,1)S(1)}) fusion(f32[2,6,128,128,8]{3,2,4,1,0:T(8,128)S(1)} %get-tuple-element.194, f32[2,8,128]{2,1,0:T(8,128)S(1)} %get-tuple-element.195, f32[2,8,128]{2,1,0:T(8,128)S(1)} %fusion.77, f32[2,8,128]{2,1,0:T(8,128)S(1)} %get-tuple-element.192, ...), kind=kLoop, calls=%fused_computation.6.clone.1 | loop fusion | flops 14155776 | bytes 18997248 | tf_op jit(solution)/shard_map/while/body/eval_jaxpr/convert_element_type | solution.py:61
  193.0 1.3 maximum_bitcast_fusion.2
  194.3 3.2 %copy.144 = f32[1,6,128,512]{3,2,1,0:T(8,128)} copy(f32[1,6,128,512]{2,3,1,0:T(8,128)} %maximum_bitcast_fusion.2) | data formatting | bytes 3145728 | tf_op jit(solution)/shard_map/while/body/jit(dynamic_update_index_in_dim)/dynamic_update_slice | solution.py:115
  197.5 2.8 %constant_dynamic-update-slice_fusion.6 = f32[4,6,128,512]{3,2,1,0:T(8,128)} fusion(f32[4,6,128,512]{3,2,1,0:T(8,128)} %get-tuple-element.215, f32[1,6,128,512]{3,2,1,0:T(8,128)} %copy.144, s32[]{:T(128)} %get-tuple-element.212), kind=kLoop, calls=%fused_computation.35.clone.1 | loop fusion | bytes 3146240 | tf_op jit(solution)/shard_map/while/body/jit(dynamic_update_index_in_dim)/dynamic_update_slice | solution.py:115
  200.3 3.5 %fusion.81 = bf16[2,128,8,128]{3,1,2,0:T(8,128)(2,1)} fusion(bf16[2,8,128,6,128]{2,4,1,3,0:T(8,128)(2,1)} %copy-done.4, bf16[6,128,2,128,1]{1,3,2,0,4:T(8,128)(2,1)} %bitcast.183), kind=kOutput, calls=%fused_computation.24.clone.1 | convolution fusion | flops 402915328 | bytes 4063232 | tf_op jit(solution)/shard_map/while/body/eval_jaxpr/grqvk,vkgd->qgrd/dot_general | solution.py:53
  203.7 2.0 copy.141
  205.8 1.4 fusion.80
  208.4 2.2 constant_dynamic-update-slice_fusion.5
  210.6 6.4 %copy.92 = f32[3,8,128,512]{3,1,2,0:T(8,128)S(1)} copy(f32[3,8,128,512]{3,2,1,0:T(8,128)} %bitcast.185) | data formatting | bytes 12582912
  217.1 2.2 convolution_convert_fusion
  219.3 1.5 convert_element_type.29
  220.8 20.5 %reduce-scatter.2.cloned.1.call-done = bf16[512,512]{1,0:T(8,128)(2,1)} async-done(((bf16[1024,512]{1,0:T(8,128)(2,1)}), bf16[512,512]{1,0:T(8,128)(2,1)}) %reduce-scatter.2.cloned.1.call-update) | async-done | bytes 524304 | tf_op jit(solution)/shard_map/reduce_scatter | solution.py:133
  241.2 1.9 fusion.36
  (155 shorter events, 49.1 us)
Async XLA Ops:
  7.2 4.7 %copy-start = (s32[8,6]{1,0:T(8,128)S(1)}, s32[8,6]{1,0:T(8,128)}, u32[]{:S(2)}) copy-start(s32[8,6]{1,0:T(8,128)} %param.15) | copy-start | bytes 580
  7.2 26.4 %all-gather.2.cloned.1.call-start = ((), (), s32[]{:S(2)}) async-start(), calls=%async_computation.1 | async-start | bytes 1572864 | tf_op jit(solution)/shard_map/all_gather | solution.py:91
  9.1 232.1 %reduce-scatter.2.cloned.1.call-start = ((), (), s32[]{:S(2)}) async-start(), calls=%async_computation.2 | async-start | bytes 1572864 | tf_op jit(solution)/shard_map/reduce_scatter | solution.py:133
  43.1 6.6 %copy-start.5 = (bf16[6,128,256]{1,2,0:T(8,128)(2,1)}, bf16[6,128,256]{1,2,0:T(8,128)(2,1)S(1)}, u32[]{:S(2)}) copy-start(bf16[6,128,256]{1,2,0:T(8,128)(2,1)S(1)} %get-tuple-element.190) | copy-start | bytes 1179652 | tf_op jit(solution)/shard_map/while
  45.7 2.6 %copy-start.1 = (f32[2,6,128,128,8]{3,2,4,1,0:T(8,128)}, f32[2,6,128,128,8]{3,2,4,1,0:T(8,128)S(1)}, u32[]{:S(2)}) copy-start(f32[2,6,128,128,8]{3,2,4,1,0:T(8,128)S(1)} %get-tuple-element.191) | copy-start | bytes 18874372 | tf_op jit(solution)/shard_map/while
  51.6 5.9 %slice-start = ((s8[6291456]{0:T(1024)(128)(4,1)}), s8[2097152]{0:T(1024)(128)(4,1)S(1)}, s32[]{:S(2)}) async-start(s8[6291456]{0:T(1024)(128)(4,1)} %bitcast.167), calls=%async_computation.3 | async-start | bytes 4194304 | tf_op jit(solution)/shard_map/while
  53.1 4.5 %slice-start.1 = ((s8[6291456]{0:T(1024)(128)(4,1)}), s8[4194304]{0:T(1024)(128)(4,1)S(1)}, s32[]{:S(2)}) async-start(s8[6291456]{0:T(1024)(128)(4,1)} %bitcast.167), calls=%async_computation.4 | async-start | bytes 8388608 | tf_op jit(solution)/shard_map/while
  60.1 1.7 copy-start.2
  60.2 2.9 %copy-start.4 = (bf16[2,8,128,6,128]{2,4,1,3,0:T(8,128)(2,1)}, bf16[2,8,128,6,128]{2,4,1,3,0:T(8,128)(2,1)S(1)}, u32[]{:S(2)}) copy-start(bf16[2,8,128,6,128]{2,4,1,3,0:T(8,128)(2,1)S(1)} %get-tuple-element.197) | copy-start | bytes 9437188 | tf_op jit(solution)/shard_map/while
  64.4 11.4 %copy-start.3 = (bf16[2,8,128,6,128]{2,4,1,3,0:T(8,128)(2,1)S(1)}, bf16[2,8,128,6,128]{2,4,1,3,0:T(8,128)(2,1)}, u32[]{:S(2)}) copy-start(bf16[2,8,128,6,128]{2,4,1,3,0:T(8,128)(2,1)} %copy-done.2) | copy-start | bytes 9437188 | tf_op jit(solution)/shard_map/while
  64.4 11.4 %copy-start.6 = (bf16[6,128,256]{1,2,0:T(8,128)(2,1)S(1)}, bf16[6,128,256]{1,2,0:T(8,128)(2,1)}, u32[]{:S(2)}) copy-start(bf16[6,128,256]{1,2,0:T(8,128)(2,1)} %copy-done.5) | copy-start | bytes 1179652 | tf_op jit(solution)/shard_map/while
  86.5 6.6 %copy-start.5 = (bf16[6,128,256]{1,2,0:T(8,128)(2,1)}, bf16[6,128,256]{1,2,0:T(8,128)(2,1)S(1)}, u32[]{:S(2)}) copy-start(bf16[6,128,256]{1,2,0:T(8,128)(2,1)S(1)} %get-tuple-element.190) | copy-start | bytes 1179652 | tf_op jit(solution)/shard_map/while
  89.1 2.6 %copy-start.1 = (f32[2,6,128,128,8]{3,2,4,1,0:T(8,128)}, f32[2,6,128,128,8]{3,2,4,1,0:T(8,128)S(1)}, u32[]{:S(2)}) copy-start(f32[2,6,128,128,8]{3,2,4,1,0:T(8,128)S(1)} %get-tuple-element.191) | copy-start | bytes 18874372 | tf_op jit(solution)/shard_map/while
  94.9 5.9 %slice-start = ((s8[6291456]{0:T(1024)(128)(4,1)}), s8[2097152]{0:T(1024)(128)(4,1)S(1)}, s32[]{:S(2)}) async-start(s8[6291456]{0:T(1024)(128)(4,1)} %bitcast.167), calls=%async_computation.3 | async-start | bytes 4194304 | tf_op jit(solution)/shard_map/while
  96.4 4.5 %slice-start.1 = ((s8[6291456]{0:T(1024)(128)(4,1)}), s8[4194304]{0:T(1024)(128)(4,1)S(1)}, s32[]{:S(2)}) async-start(s8[6291456]{0:T(1024)(128)(4,1)} %bitcast.167), calls=%async_computation.4 | async-start | bytes 8388608 | tf_op jit(solution)/shard_map/while
  103.5 1.7 copy-start.2
  103.5 2.9 %copy-start.4 = (bf16[2,8,128,6,128]{2,4,1,3,0:T(8,128)(2,1)}, bf16[2,8,128,6,128]{2,4,1,3,0:T(8,128)(2,1)S(1)}, u32[]{:S(2)}) copy-start(bf16[2,8,128,6,128]{2,4,1,3,0:T(8,128)(2,1)S(1)} %get-tuple-element.197) | copy-start | bytes 9437188 | tf_op jit(solution)/shard_map/while
  107.7 11.4 %copy-start.3 = (bf16[2,8,128,6,128]{2,4,1,3,0:T(8,128)(2,1)S(1)}, bf16[2,8,128,6,128]{2,4,1,3,0:T(8,128)(2,1)}, u32[]{:S(2)}) copy-start(bf16[2,8,128,6,128]{2,4,1,3,0:T(8,128)(2,1)} %copy-done.2) | copy-start | bytes 9437188 | tf_op jit(solution)/shard_map/while
  107.7 11.4 %copy-start.6 = (bf16[6,128,256]{1,2,0:T(8,128)(2,1)S(1)}, bf16[6,128,256]{1,2,0:T(8,128)(2,1)}, u32[]{:S(2)}) copy-start(bf16[6,128,256]{1,2,0:T(8,128)(2,1)} %copy-done.5) | copy-start | bytes 1179652 | tf_op jit(solution)/shard_map/while
  129.8 6.6 %copy-start.5 = (bf16[6,128,256]{1,2,0:T(8,128)(2,1)}, bf16[6,128,256]{1,2,0:T(8,128)(2,1)S(1)}, u32[]{:S(2)}) copy-start(bf16[6,128,256]{1,2,0:T(8,128)(2,1)S(1)} %get-tuple-element.190) | copy-start | bytes 1179652 | tf_op jit(solution)/shard_map/while
  132.4 2.6 %copy-start.1 = (f32[2,6,128,128,8]{3,2,4,1,0:T(8,128)}, f32[2,6,128,128,8]{3,2,4,1,0:T(8,128)S(1)}, u32[]{:S(2)}) copy-start(f32[2,6,128,128,8]{3,2,4,1,0:T(8,128)S(1)} %get-tuple-element.191) | copy-start | bytes 18874372 | tf_op jit(solution)/shard_map/while
  138.3 5.9 %slice-start = ((s8[6291456]{0:T(1024)(128)(4,1)}), s8[2097152]{0:T(1024)(128)(4,1)S(1)}, s32[]{:S(2)}) async-start(s8[6291456]{0:T(1024)(128)(4,1)} %bitcast.167), calls=%async_computation.3 | async-start | bytes 4194304 | tf_op jit(solution)/shard_map/while
  139.7 4.5 %slice-start.1 = ((s8[6291456]{0:T(1024)(128)(4,1)}), s8[4194304]{0:T(1024)(128)(4,1)S(1)}, s32[]{:S(2)}) async-start(s8[6291456]{0:T(1024)(128)(4,1)} %bitcast.167), calls=%async_computation.4 | async-start | bytes 8388608 | tf_op jit(solution)/shard_map/while
  146.8 1.7 copy-start.2
  146.8 2.9 %copy-start.4 = (bf16[2,8,128,6,128]{2,4,1,3,0:T(8,128)(2,1)}, bf16[2,8,128,6,128]{2,4,1,3,0:T(8,128)(2,1)S(1)}, u32[]{:S(2)}) copy-start(bf16[2,8,128,6,128]{2,4,1,3,0:T(8,128)(2,1)S(1)} %get-tuple-element.197) | copy-start | bytes 9437188 | tf_op jit(solution)/shard_map/while
  151.0 11.4 %copy-start.3 = (bf16[2,8,128,6,128]{2,4,1,3,0:T(8,128)(2,1)S(1)}, bf16[2,8,128,6,128]{2,4,1,3,0:T(8,128)(2,1)}, u32[]{:S(2)}) copy-start(bf16[2,8,128,6,128]{2,4,1,3,0:T(8,128)(2,1)} %copy-done.2) | copy-start | bytes 9437188 | tf_op jit(solution)/shard_map/while
  151.0 11.4 %copy-start.6 = (bf16[6,128,256]{1,2,0:T(8,128)(2,1)S(1)}, bf16[6,128,256]{1,2,0:T(8,128)(2,1)}, u32[]{:S(2)}) copy-start(bf16[6,128,256]{1,2,0:T(8,128)(2,1)} %copy-done.5) | copy-start | bytes 1179652 | tf_op jit(solution)/shard_map/while
  173.1 6.6 %copy-start.5 = (bf16[6,128,256]{1,2,0:T(8,128)(2,1)}, bf16[6,128,256]{1,2,0:T(8,128)(2,1)S(1)}, u32[]{:S(2)}) copy-start(bf16[6,128,256]{1,2,0:T(8,128)(2,1)S(1)} %get-tuple-element.190) | copy-start | bytes 1179652 | tf_op jit(solution)/shard_map/while
  175.7 2.6 %copy-start.1 = (f32[2,6,128,128,8]{3,2,4,1,0:T(8,128)}, f32[2,6,128,128,8]{3,2,4,1,0:T(8,128)S(1)}, u32[]{:S(2)}) copy-start(f32[2,6,128,128,8]{3,2,4,1,0:T(8,128)S(1)} %get-tuple-element.191) | copy-start | bytes 18874372 | tf_op jit(solution)/shard_map/while
  181.6 5.9 %slice-start = ((s8[6291456]{0:T(1024)(128)(4,1)}), s8[2097152]{0:T(1024)(128)(4,1)S(1)}, s32[]{:S(2)}) async-start(s8[6291456]{0:T(1024)(128)(4,1)} %bitcast.167), calls=%async_computation.3 | async-start | bytes 4194304 | tf_op jit(solution)/shard_map/while
  183.0 4.5 %slice-start.1 = ((s8[6291456]{0:T(1024)(128)(4,1)}), s8[4194304]{0:T(1024)(128)(4,1)S(1)}, s32[]{:S(2)}) async-start(s8[6291456]{0:T(1024)(128)(4,1)} %bitcast.167), calls=%async_computation.4 | async-start | bytes 8388608 | tf_op jit(solution)/shard_map/while
  190.1 1.7 copy-start.2
  190.1 2.9 %copy-start.4 = (bf16[2,8,128,6,128]{2,4,1,3,0:T(8,128)(2,1)}, bf16[2,8,128,6,128]{2,4,1,3,0:T(8,128)(2,1)S(1)}, u32[]{:S(2)}) copy-start(bf16[2,8,128,6,128]{2,4,1,3,0:T(8,128)(2,1)S(1)} %get-tuple-element.197) | copy-start | bytes 9437188 | tf_op jit(solution)/shard_map/while
  194.3 11.5 %copy-start.3 = (bf16[2,8,128,6,128]{2,4,1,3,0:T(8,128)(2,1)S(1)}, bf16[2,8,128,6,128]{2,4,1,3,0:T(8,128)(2,1)}, u32[]{:S(2)}) copy-start(bf16[2,8,128,6,128]{2,4,1,3,0:T(8,128)(2,1)} %copy-done.2) | copy-start | bytes 9437188 | tf_op jit(solution)/shard_map/while
  194.3 11.5 %copy-start.6 = (bf16[6,128,256]{1,2,0:T(8,128)(2,1)S(1)}, bf16[6,128,256]{1,2,0:T(8,128)(2,1)}, u32[]{:S(2)}) copy-start(bf16[6,128,256]{1,2,0:T(8,128)(2,1)} %copy-done.5) | copy-start | bytes 1179652 | tf_op jit(solution)/shard_map/while
  210.6 6.4 %copy-start.7 = (s32[24]{0:T(128)S(1)}, s32[24]{0:T(128)}, u32[]{:S(2)}) copy-start(s32[24]{0:T(128)} %eq.16) | copy-start | bytes 292
Sparse Core Ops, SparseCore 0:
  9.6 23.9 all-gather.1
  220.9 20.3 reduce-scatter.1
where the time goes:
time: 252 us; the launch traced here: 250 us
  local copies, waits for them, and re-layouts  110 us (44%)
  matrix products  53 us (21%)
  waiting for transfers between devices  42.2 us (17%)
  other arithmetic  29.7 us (12%)
  between operations  14.1 us (6%)
    dynamic_update_slice x20, local copies, waits for them, and re-layouts, body(): lax.map(one_block, (query_states.reshape(per_shard, MASK_BLOCK_SIZE, -1),...  45.6 us
    dynamic_slice x32, local copies, waits for them, and re-layouts, body(): lax.map(one_block, (query_states.reshape(per_shard, MASK_BLOCK_SIZE, -1),...  33.1 us
    all_gather x1, waiting for transfers between devices, body(): gathered = lax.all_gather(local_kv, 'ctx', axis=0, tiled=True)  21.7 us
    reduce_scatter x1, waiting for transfers between devices, body(): lax.psum_scatter(dense_part.reshape(total_blocks * MASK_BLOCK_SIZE, kv_to...  20.5 us
    dot_general x4, matrix products, attend(): jnp.einsum('qgrd,vkgd->grqvk', output_gradients, value_portion, preferred...  17.8 us
    dot_general x4, matrix products, attend(): jnp.einsum('grqvk,vkgd->qgrd', probs_low, value_portion, preferred_elemen...  13.8 us
    while x64, local copies, waits for them, and re-layouts  12.6 us
    convert_element_type x4, other arithmetic, attend(): (soft_probs * (dprobs - row_delta) * inv_root).astype(jnp.bfloat16)  10.3 us
  transfers between devices with their start and end apart: 2, of which 2 were waited for; matrix products, arithmetic and copies ran while one was open for 1% of the time, Pallas kernels for 0%

commit v1 on v0

v1 whole, which is shorter than its diff:
```python
import functools
import math

import jax
import jax.numpy as jnp
from jax import lax
from jax.experimental import pallas as pl
from jax.experimental.pallas import tpu as pltpu
from jax.sharding import PartitionSpec as P

HEAD_SIZE = 128
BLOCK = 128
CAP = 2
CHUNK = 2
MASKED = -1e30
INV_ROOT = 1.0 / math.sqrt(HEAD_SIZE)
EXP2_SCALE = INV_ROOT * math.log2(math.e)
SMALL_VMEM = 8 * 1024 * 1024
LARGE_VMEM = 16 * 1024 * 1024


def dot(a, b, contract):
    return lax.dot_general(a, b, (contract, ((), ())), preferred_element_type=jnp.float32)


def split(block, per_shard):
    if per_shard & (per_shard - 1) == 0:
        return block >> (per_shard.bit_length() - 1), block & (per_shard - 1)
    return lax.div(block, jnp.int32(per_shard)), lax.rem(block, jnp.int32(per_shard))


def rank_of(bits, index):
    below = bits & ((jnp.int32(1) << index) - 1)
    return jnp.where(below != 0, 1, 0).astype(jnp.int32)


def plan_width(vis):
    return 2 * vis + 1


def plan_size(ctx_size, per_shard, vis):
    return 2 * per_shard * plan_width(vis) + ctx_size - 1


def reader_bits(ctx_size, per_shard, vis):
    return 2 * per_shard * plan_width(vis)


def pack_kernel(
    ctx_size, per_shard, vis, blocks_ref, count_ref, lens_ref, k_ref, v_ref, out_ref, plan_ref, bits_ref, sem
):
    me = lax.axis_index("ctx")
    bits_at = reader_bits(ctx_size, per_shard, vis)

    def each_copy(act):
        for shift in range(1, ctx_size):
            bits = plan_ref[bits_at + shift - 1]
            for index in range(per_shard):

                @pl.when((bits >> index) & 1 == 1)
                def _():
                    rows = pl.ds(index * BLOCK, BLOCK)
                    to = pl.ds(pl.multiple_of(rank_of(bits, jnp.int32(index)) * BLOCK, BLOCK), BLOCK)
                    for part, ref in enumerate((k_ref, v_ref)):
                        act(
                            pltpu.make_async_copy(
                                ref.at[rows, :], out_ref.at[part, shift - 1, to, :], sem.at[shift - 1, index, part]
                            )
                        )

    for shift in range(1, ctx_size):
        reader = me + shift
        plan_ref[bits_at + shift - 1] = jnp.int32(0)

        @pl.when(reader < ctx_size)
        def _():
            bits = jnp.int32(0)
            for row in range(per_shard):
                at = reader * per_shard + row
                count = count_ref[at]
                for slot in range(1, vis):
                    owner, index = split(blocks_ref[at, slot], per_shard)
                    bits = bits | jnp.where((slot < count) & (owner == me), jnp.int32(1) << index, 0)
            plan_ref[bits_at + shift - 1] = bits

    each_copy(lambda copy: copy.start())
    for row in range(per_shard):
        at = me * per_shard + row
        count = count_ref[at]
        near_at = row * plan_width(vis)
        near = jnp.int32(0)
        for slot in range(vis):
            owner, index = split(blocks_ref[at, slot], per_shard)
            plan_ref[near_at + 1 + near] = index
            plan_ref[near_at + 1 + vis + near] = lens_ref[at, slot]
            near = near + ((slot < count) & (owner == me)).astype(jnp.int32)
        plan_ref[near_at] = near
        plan_ref[(per_shard + row) * plan_width(vis)] = jnp.int32(0)

    @pl.when(me > 0)
    def _():
        for owner in range(ctx_size):
            bits_ref[owner] = jnp.int32(0)
        for row in range(per_shard):
            at = me * per_shard + row
            count = count_ref[at]
            for slot in range(1, vis):
                owner, index = split(blocks_ref[at, slot], per_shard)
                bits_ref[owner] = bits_ref[owner] | jnp.where(slot < count, jnp.int32(1) << index, 0)
        for row in range(per_shard):
            at = me * per_shard + row
            count = count_ref[at]
            far_at = (per_shard + row) * plan_width(vis)
            far = jnp.int32(0)
            for slot in range(1, vis):
                owner, index = split(blocks_ref[at, slot], per_shard)
                plan_ref[far_at + 1 + far] = CAP * (me - owner - 1) + rank_of(bits_ref[owner], index)
                plan_ref[far_at + 1 + vis + far] = lens_ref[at, slot]
                far = far + ((slot < count) & (owner != me)).astype(jnp.int32)
            plan_ref[far_at] = far

    each_copy(lambda copy: copy.wait())


def add_kernel(ctx_size, per_shard, vis, plan_ref, own_ref, recv_ref, dk_ref, dv_ref, gk_ref, gv_ref, total_ref, sem):
    del dk_ref, dv_ref
    bits_at = reader_bits(ctx_size, per_shard, vis)
    every = jnp.int32(0)
    for shift in range(1, ctx_size):
        every = every | plan_ref[bits_at + shift - 1]

    def each_block(act):
        for index in range(per_shard):

            @pl.when((every >> index) & 1 == 1)
            def _():
                rows = pl.ds(index * BLOCK, BLOCK)
                for part, dst in enumerate((gk_ref, gv_ref)):
                    act(
                        index, part, rows,
                        pltpu.make_async_copy(total_ref.at[part, rows, :], dst.at[rows, :], sem.at[part, index]),
                    )

    def add(index, part, rows, write):
        def step(s, acc):
            bits = plan_ref[bits_at + s]
            use = (bits >> index) & 1
            to = pl.multiple_of(rank_of(bits, jnp.int32(index)) * BLOCK, BLOCK)
            got = recv_ref[part, s, pl.ds(to, BLOCK), :].astype(jnp.float32)
            return acc + jnp.where(use == 1, got, 0.0)

        total = lax.fori_loop(0, ctx_size - 1, step, own_ref[part, rows, :].astype(jnp.float32))
        total_ref[part, rows, :] = total.astype(jnp.bfloat16)
        write.start()

    each_block(add)
    each_block(lambda index, part, rows, write: write.wait())


def both(first, then):
    def stage(i):
        first(i)
        then(i)

    return stage


def skewed(parts, stages):
    for tick in range(parts + len(stages) - 1):
        for k in reversed(range(len(stages))):
            if 0 <= tick - k < parts:
                stages[k](tick - k)


def rows_of_heads(ref, rows, lanes):
    return jnp.concatenate([ref[rows, l] for l in lanes], axis=0)


def store_heads(ref, rows, lanes, value):
    for i, l in enumerate(lanes):
        ref[rows, l] = value[i * BLOCK : (i + 1) * BLOCK]


def hide(masks, scores):
    return jnp.concatenate(
        [jnp.where(m, scores[:, i * BLOCK : (i + 1) * BLOCK], MASKED) for i, m in enumerate(masks)], axis=1
    )


def head_lanes(width):
    parts = width // (CHUNK * HEAD_SIZE)
    return [[pl.ds((CHUNK * c + i) * HEAD_SIZE, HEAD_SIZE) for i in range(CHUNK)] for c in range(parts)]


def chunk_rows(c):
    return pl.ds(c * CHUNK * BLOCK, CHUNK * BLOCK)


def table_rows(ref, g, pos):
    lanes = pl.ds(g * HEAD_SIZE, HEAD_SIZE)
    return jnp.concatenate([ref[pl.ds(pl.multiple_of(p * BLOCK, BLOCK), BLOCK), lanes] for p in pos], axis=0)


def with_ones(values):
    return jnp.concatenate([values, jnp.ones_like(values)], axis=1)


def table_lanes(ref, g, pos):
    return jnp.concatenate([ref[g, p] for p in pos], axis=1)


def accumulate(acc, g, pos, total):
    for i, p in enumerate(pos):
        acc[g, p] += total[:, i * BLOCK : (i + 1) * BLOCK]


def add_to(total, key, value):
    total[key] = total[key] + value if key in total else value


def iotas(chunk):
    shape = (chunk * BLOCK, BLOCK)
    return lax.broadcasted_iota(jnp.int32, shape, 0) % BLOCK, lax.broadcasted_iota(jnp.int32, shape, 1)


def far_masks(chunk, lens):
    _, key_at = iotas(chunk)
    return [key_at < n for n in lens]


def hidden_bias(masks):
    return jnp.concatenate([jnp.where(m, 0.0, MASKED) for m in masks], axis=1).astype(jnp.bfloat16)


def near_lengths(ctx_size, per_shard, vis, blocks_ref, count_ref, lens_ref):
    me = lax.axis_index("ctx")
    lengths = []
    for row in range(per_shard):
        at = me * per_shard + row
        count = count_ref[at]
        slots = [(blocks_ref[at, s], lens_ref[at, s], s < count) for s in range(1, vis)] if row else []
        of_row = []
        for earlier in range(row):
            length = jnp.int32(0)
            for block, visible, live in slots:
                length = length + jnp.where(live & (block == me * per_shard + earlier), visible, 0)
            of_row.append(length)
        lengths.append(of_row)
    return lengths


def near_masks(chunk, lengths):
    query_at, key_at = iotas(chunk)
    return [key_at < n for n in lengths] + [key_at <= query_at]


def block_rows(row):
    return pl.ds(row * BLOCK, BLOCK)


def forward_kernel(
    ctx_size, per_shard, vis, blocks_ref, count_ref, lens_ref, q_ref, k_ref, v_ref, part_ref, top_ref, norm_ref, p_ref
):
    kv_heads = k_ref.shape[1] // HEAD_SIZE
    lanes = head_lanes(q_ref.shape[1])
    parts = len(lanes)
    lengths = near_lengths(ctx_size, per_shard, vis, blocks_ref, count_ref, lens_ref)
    biases = [hidden_bias(near_masks(1, of_row)) for of_row in lengths]
    query_at, lane_at = iotas(CHUNK)
    which = jnp.where(query_at == lane_at, 1.0, 0.0).astype(jnp.bfloat16)
    heads_at = [pl.ds(g * HEAD_SIZE, HEAD_SIZE) for g in range(kv_heads)]
    k_t = [k_ref[:, at].T for at in heads_at]
    k_bias = [[jnp.concatenate([x[:, : bias.shape[1]], bias], axis=0) for x in k_t] for bias in biases]
    v_one = [with_ones(v_ref[:, at]) for at in heads_at]
    chunks = [(row, c, c * kv_heads // parts) for row in range(per_shard) for c in range(parts)]
    scores, weights, summed = ([None] * len(chunks) for _ in range(3))

    def stage_scores(i):
        row, c, g = chunks[i]
        q = rows_of_heads(q_ref, block_rows(row), lanes[c])
        scores[i] = dot(jnp.concatenate([q, which], axis=1), k_bias[row][g], ((1,), (0,)))

    def stage_weights(i):
        row, c, g = chunks[i]
        seen = scores[i]
        top = jnp.ceil(jnp.max(seen, axis=1, keepdims=True) * EXP2_SCALE)
        weights[i] = jnp.exp2(seen * EXP2_SCALE - top).astype(jnp.bfloat16)
        p_ref[row, chunk_rows(c), pl.ds(0, (row + 1) * BLOCK)] = weights[i]
        store_heads(top_ref, block_rows(row), lanes[c], jnp.broadcast_to(top, (CHUNK * BLOCK, HEAD_SIZE)))

    def stage_summed(i):
        row, c, g = chunks[i]
        summed[i] = dot(weights[i], v_one[g][: (row + 1) * BLOCK], ((1,), (0,)))

    def stage_out(i):
        row, c, g = chunks[i]
        store_heads(part_ref, block_rows(row), lanes[c], summed[i][:, :HEAD_SIZE])
        store_heads(norm_ref, block_rows(row), lanes[c], summed[i][:, HEAD_SIZE:])

    skewed(len(chunks), [stage_scores, stage_weights, stage_summed, stage_out])


def backward_kernel(
    ctx_size, per_shard, vis, q_ref, go_ref, dq_far_ref, delta_ref, p_ref, k_ref, v_ref, att_ref, *rest
):
    own_ref, o_ref, dq_ref, dk_ref, dv_ref, acc_k, acc_v, dq_rows, sem = rest[-9:]
    kv_heads = k_ref.shape[1] // HEAD_SIZE
    lanes = head_lanes(q_ref.shape[1])
    parts = len(lanes)
    heads_at = [pl.ds(g * HEAD_SIZE, HEAD_SIZE) for g in range(kv_heads)]
    copies = [pltpu.make_async_copy(att_ref, o_ref, sem.at[0])]
    copies[0].start()
    v_t = [v_ref[:, at].T for at in heads_at]
    order = list(reversed(range(per_shard)))
    chunks = [(row, c, c * kv_heads // parts) for row in order for c in range(parts)]
    go, dprobs, weights, dscores = ([None] * len(chunks) for _ in range(4))
    total_v, total_k = {}, {}

    def stage_dprobs(i):
        row, c, g = chunks[i]
        go[i] = rows_of_heads(go_ref, block_rows(row), lanes[c])
        dprobs[i] = dot(go[i], v_t[g][:, : (row + 1) * BLOCK], ((1,), (0,)))

    def stage_dscores(i):
        row, c, g = chunks[i]
        delta = repeat(rows_of_heads(delta_ref, block_rows(row), lanes[c]), row + 1)
        weights[i] = p_ref[row, chunk_rows(c), pl.ds(0, (row + 1) * BLOCK)]
        dscores[i] = weights[i] * (dprobs[i] - delta).astype(jnp.bfloat16)

    def stage_grads(i):
        row, c, g = chunks[i]
        dq = dot(dscores[i], k_ref[pl.ds(0, (row + 1) * BLOCK), heads_at[g]], ((1,), (0,)))
        dq = dq + rows_of_heads(dq_far_ref, block_rows(row), lanes[c])
        store_heads(dq_rows, block_rows(row), lanes[c], (dq * INV_ROOT).astype(jnp.bfloat16))
        add_to(total_v, (row, g), dot(go[i], weights[i], ((0,), (0,))))
        add_to(total_k, (row, g), dot(rows_of_heads(q_ref, block_rows(row), lanes[c]), dscores[i], ((0,), (0,))))
        if (c + 1) * kv_heads // parts == g + 1:
            settle(row, g)
        if c == parts - 1:
            copy = pltpu.make_async_copy(
                dq_rows.at[block_rows(row), :], dq_ref.at[block_rows(row), :], sem.at[1 + row]
            )
            copy.start()
            copies.append(copy)

    def settle(row, g):
        for total, acc, part, scale in ((total_k, acc_k, 0, INV_ROOT), (total_v, acc_v, 1, None)):
            value = total[row, g]
            if row < per_shard - 1:
                value = value + acc[g, :, pl.ds(0, (row + 1) * BLOCK)]
            if row:
                acc[g, :, pl.ds(0, row * BLOCK)] = value[:, : row * BLOCK]
            done = value[:, row * BLOCK :]
            done = (done if scale is None else done * scale).astype(jnp.bfloat16).T
            own_ref[part, block_rows(row), heads_at[g]] = done

    skewed(len(chunks), [stage_dprobs, stage_dscores, stage_grads])
    for part, dst in enumerate((dk_ref, dv_ref)):
        copy = pltpu.make_async_copy(own_ref.at[part], dst, sem.at[1 + per_shard + part])
        copy.start()
        copies.append(copy)
    for copy in copies:
        copy.wait()


def finish(rows, lanes, go_ref, out, inv_norm, near, o_ref, go_near_ref, delta_ref):
    store_heads(o_ref, rows, lanes, out.astype(jnp.bfloat16))
    scaled = (rows_of_heads(go_ref, rows, lanes).astype(jnp.float32) * inv_norm).astype(jnp.bfloat16)
    exact = scaled.astype(jnp.float32)
    delta = jnp.sum(exact * out, axis=1, keepdims=True)
    if near is None:
        store_heads(go_near_ref, rows, lanes, scaled)
        store_heads(delta_ref, rows, lanes, jnp.broadcast_to(delta, out.shape))
    else:
        store_heads(go_near_ref, rows, lanes, (exact * near).astype(jnp.bfloat16))
        store_heads(delta_ref, rows, lanes, delta * near)
    return scaled, delta


def only_local(rows, lanes, go_ref, part_ref, norm_ref, o_ref, go_near_ref, delta_ref):
    for of in lanes:
        inv_norm = 1.0 / rows_of_heads(norm_ref, rows, of)
        out = rows_of_heads(part_ref, rows, of) * inv_norm
        finish(rows, of, go_ref, out, inv_norm, None, o_ref, go_near_ref, delta_ref)


def repeat(value, times):
    return jnp.concatenate([value] * times, axis=1)


def with_far(
    slots, kv_heads, rows, q_ref, go_ref, part_ref, top_ref, norm_ref, far_ref, o_ref, dq_ref, go_near_ref, delta_ref,
    kt_t, vt_t, acc_k, acc_v, pos, lens,
):
    lanes = head_lanes(q_ref.shape[1])
    parts = len(lanes)
    kv = [c * kv_heads // parts for c in range(parts)]
    masks = far_masks(CHUNK, lens)
    k_cat = [table_rows(far_ref.at[0], g, pos) for g in range(kv_heads)]
    v_one = [with_ones(table_rows(far_ref.at[1], g, pos)) for g in range(kv_heads)]
    k_cat_t = [table_lanes(kt_t, g, pos) for g in range(kv_heads)]
    v_cat_t = [table_lanes(vt_t, g, pos) for g in range(kv_heads)]
    q, scores, top, near, weights, summed, scaled, delta, dprobs, dscores = ([None] * parts for _ in range(10))
    total_v, total_k = {}, {}

    def stage_scores(c):
        q[c] = rows_of_heads(q_ref, rows, lanes[c])
        scores[c] = dot(q[c], k_cat_t[kv[c]], ((1,), (0,)))

    def stage_weights(c):
        seen = hide(masks, scores[c])
        top_near = rows_of_heads(top_ref, rows, lanes[c])
        top[c] = jnp.maximum(jnp.ceil(jnp.max(seen, axis=1, keepdims=True) * EXP2_SCALE), top_near)
        near[c] = jnp.exp2(top_near - top[c])
        weights[c] = jnp.exp2(seen * EXP2_SCALE - repeat(top[c], slots)).astype(jnp.bfloat16)

    def stage_summed(c):
        summed[c] = dot(weights[c], v_one[kv[c]], ((1,), (0,)))

    def stage_out(c):
        inv_norm = 1.0 / (near[c] * rows_of_heads(norm_ref, rows, lanes[c]) + summed[c][:, HEAD_SIZE:])
        out = (rows_of_heads(part_ref, rows, lanes[c]) * near[c] + summed[c][:, :HEAD_SIZE]) * inv_norm
        scaled[c], delta[c] = finish(rows, lanes[c], go_ref, out, inv_norm, near[c], o_ref, go_near_ref, delta_ref)

    def stage_dprobs(c):
        dprobs[c] = dot(scaled[c], v_cat_t[kv[c]], ((1,), (0,)))

    def stage_dscores(c):
        dscores[c] = (weights[c] * (dprobs[c] - delta[c]).astype(jnp.bfloat16))

    def stage_grads(c):
        store_heads(dq_ref, rows, lanes[c], dot(dscores[c], k_cat[kv[c]], ((1,), (0,))))
        add_to(total_v, kv[c], dot(scaled[c], weights[c], ((0,), (0,))))
        add_to(total_k, kv[c], dot(q[c], dscores[c], ((0,), (0,))))

    skewed(
        parts,
        [stage_scores, stage_weights, stage_summed, stage_out, stage_dprobs, stage_dscores, stage_grads],
    )
    for g in range(kv_heads):
        accumulate(acc_v, g, pos, total_v[g])
        accumulate(acc_k, g, pos, total_k[g])


def flip_table(src, dst, kv_heads, count):
    for g in range(kv_heads):
        for i in range(count):
            dst[g, i] = src[pl.ds(i * BLOCK, BLOCK), pl.ds(g * HEAD_SIZE, HEAD_SIZE)].T


def flush(acc, dst, kv_heads, count, scale):
    for g in range(kv_heads):
        for i in range(count):
            value = acc[g, i] if scale is None else acc[g, i] * scale
            dst[pl.ds(i * BLOCK, BLOCK), pl.ds(g * HEAD_SIZE, HEAD_SIZE)] = value.astype(jnp.bfloat16).T


def step_rows():
    row = pl.program_id(0)
    return row, pl.ds(pl.multiple_of(row * BLOCK, BLOCK), BLOCK)


def for_slots(plan_ref, at, most, vis, run):
    size = plan_ref[at]
    for slots in range(1, most + 1):

        @pl.when(size == slots)
        def _():
            pos = [plan_ref[at + 1 + slot] for slot in range(slots)]
            lens = [plan_ref[at + 1 + vis + slot] for slot in range(slots)]
            run(slots, pos, lens)


def far_kernel(
    ctx_size, per_shard, vis, plan_ref, q_ref, go_ref, part_ref, top_ref, norm_ref, far_ref,
    o_ref, dq_ref, delta_ref, go_near_ref, dfar_ref, kt_t, vt_t, acc_k, acc_v,
):
    row, rows = step_rows()
    far = CAP * (ctx_size - 1)
    kv_heads = far_ref.shape[2] // HEAD_SIZE
    at = (per_shard + row) * plan_width(vis)

    @pl.when(row == 0)
    def _():
        flip_table(far_ref.at[0], kt_t, kv_heads, far)
        flip_table(far_ref.at[1], vt_t, kv_heads, far)
        acc_k[...] = jnp.zeros_like(acc_k)
        acc_v[...] = jnp.zeros_like(acc_v)

    @pl.when(plan_ref[at] == 0)
    def _():
        only_local(rows, head_lanes(go_ref.shape[1]), go_ref, part_ref, norm_ref, o_ref, go_near_ref, delta_ref)
        dq_ref[rows, :] = jnp.zeros((BLOCK, dq_ref.shape[1]), dq_ref.dtype)

    def run(slots, pos, lens):
        with_far(
            slots, kv_heads, rows, q_ref, go_ref, part_ref, top_ref, norm_ref, far_ref, o_ref, dq_ref, go_near_ref, delta_ref,
            kt_t, vt_t, acc_k, acc_v, pos, lens,
        )

    for_slots(plan_ref, at, min(vis - 1, far), vis, run)

    @pl.when(row == pl.num_programs(0) - 1)
    def _():
        flush(acc_k, dfar_ref.at[0], kv_heads, far, INV_ROOT)
        flush(acc_v, dfar_ref.at[1], kv_heads, far, None)


def far_blocks(per_shard, vis, blocks_ref, count_ref, reader, owner):
    first, second = jnp.int32(per_shard), jnp.int32(-1)
    for row in range(per_shard):
        at = reader * per_shard + row
        count = count_ref[at]
        for slot in range(1, vis):
            of, index = split(blocks_ref[at, slot], per_shard)
            take = (slot < count) & (of == owner)
            first = jnp.minimum(first, jnp.where(take, index, per_shard))
            second = jnp.maximum(second, jnp.where(take, index, -1))
    return jnp.minimum(first, per_shard - 1), jnp.maximum(second, 0), second >= 0


def pack_pair_kernel(per_shard, vis, blocks_ref, count_ref, k_ref, v_ref, *rest):
    *out_refs, wide_ref, sem = rest
    me = lax.axis_index("ctx")

    @pl.when(me == 0)
    def _():
        first, second, _ = far_blocks(per_shard, vis, blocks_ref, count_ref, 1, 0)
        copies = []
        for place, index in enumerate((first, second)):
            rows = pl.ds(pl.multiple_of(index * BLOCK, BLOCK), BLOCK)
            for part, ref in enumerate((k_ref, v_ref)):
                copies.append(
                    pltpu.make_async_copy(
                        ref.at[rows, :], wide_ref.at[part, block_rows(place), :], sem.at[place, part]
                    )
                )
        for copy in copies:
            copy.start()
        for copy in copies:
            copy.wait()
        for g, out_ref in enumerate(out_refs):
            out_ref[:, 0] = wide_ref[:, :, pl.ds(g * HEAD_SIZE, HEAD_SIZE)]


def add_pair_kernel(
    per_shard, vis, blocks_ref, count_ref, own_ref, *rest
):
    *recv_refs, _, _, gk_ref, gv_ref, total_ref, sem = rest

    @pl.when(lax.axis_index("ctx") == 0)
    def _():
        first, second, _ = far_blocks(per_shard, vis, blocks_ref, count_ref, 1, 0)
        same = first == second
        copies = []
        for place, index in enumerate((first, second)):
            rows = pl.ds(pl.multiple_of(index * BLOCK, BLOCK), BLOCK)
            for part, dst in enumerate((gk_ref, gv_ref)):
                for g, recv_ref in enumerate(recv_refs):
                    lanes = pl.ds(g * HEAD_SIZE, HEAD_SIZE)
                    got = [recv_ref[part, 0, block_rows(p), :].astype(jnp.float32) for p in (place, 1 - place)]
                    total = own_ref[part, rows, lanes].astype(jnp.float32) + got[0] + jnp.where(same, got[1], 0.0)
                    total_ref[part, block_rows(place), lanes] = total.astype(jnp.bfloat16)
                copy = pltpu.make_async_copy(
                    total_ref.at[part, block_rows(place), :], dst.at[rows, :], sem.at[place, part]
                )
                copies.append((place, copy))

        def each(act):
            for place, copy in copies:
                if place == 0:
                    act(copy)
                else:
                    pl.when(jnp.logical_not(same))(functools.partial(act, copy))

        each(lambda copy: copy.start())
        each(lambda copy: copy.wait())


def far_pair_kernel(
    per_shard, vis, kv_heads, g, blocks_ref, count_ref, lens_ref, q_ref, go_ref, part_ref, top_ref, norm_ref, far_ref,
    *rest
):
    o_ref, dq_ref, delta_ref, go_near_ref, dfar_ref = rest[-5:]
    me = lax.axis_index("ctx")
    lanes = head_lanes(q_ref.shape[1])
    per_kv = len(lanes) // kv_heads
    lanes = lanes[g * per_kv : (g + 1) * per_kv]
    all_lanes = pl.ds(g * per_kv * CHUNK * HEAD_SIZE, per_kv * CHUNK * HEAD_SIZE)
    first, second, some = far_blocks(per_shard, vis, blocks_ref, count_ref, me, me - 1)

    @pl.when(jnp.logical_not(some))
    def _():
        for row in range(per_shard):
            only_local(block_rows(row), lanes, go_ref, part_ref, norm_ref, o_ref, go_near_ref, delta_ref)
        dq_ref[:, all_lanes] = jnp.zeros((dq_ref.shape[0], all_lanes.size), dq_ref.dtype)
        dfar_ref[...] = jnp.zeros_like(dfar_ref)

    @pl.when(some)
    def _():
        earlier = (me - 1) * per_shard
        masks = []
        for row in range(per_shard):
            at = me * per_shard + row
            count = count_ref[at]
            lens = [jnp.int32(0), jnp.int32(0)]
            for slot in range(1, vis):
                block, visible = blocks_ref[at, slot], lens_ref[at, slot]
                live = slot < count
                lens[0] = lens[0] + jnp.where(live & (block == earlier + first), visible, 0)
                lens[1] = lens[1] + jnp.where(live & (block == earlier + second) & (first != second), visible, 0)
            masks.append(far_masks(CHUNK, lens))
        k, v = far_ref[0], far_ref[1]
        k_t, v_t, v_one = k.T, v.T, with_ones(v)
        chunks = [(row, c) for row in range(per_shard) for c in range(per_kv)]
        q, scores, top, near, weights, summed, scaled, delta, dprobs, dscores = (
            [None] * len(chunks) for _ in range(10)
        )
        total = {}

        def stage_scores(i):
            row, c = chunks[i]
            q[i] = rows_of_heads(q_ref, block_rows(row), lanes[c])
            scores[i] = dot(q[i], k_t, ((1,), (0,)))

        def stage_weights(i):
            row, c = chunks[i]
            seen = hide(masks[row], scores[i])
            top_near = rows_of_heads(top_ref, block_rows(row), lanes[c])
            top[i] = jnp.maximum(jnp.ceil(jnp.max(seen, axis=1, keepdims=True) * EXP2_SCALE), top_near)
            near[i] = jnp.exp2(top_near - top[i])
            weights[i] = jnp.exp2(seen * EXP2_SCALE - repeat(top[i], CAP)).astype(jnp.bfloat16)

        def stage_summed(i):
            summed[i] = dot(weights[i], v_one, ((1,), (0,)))

        def stage_out(i):
            row, c = chunks[i]
            rows = block_rows(row)
            inv_norm = 1.0 / (near[i] * rows_of_heads(norm_ref, rows, lanes[c]) + summed[i][:, HEAD_SIZE:])
            out = (rows_of_heads(part_ref, rows, lanes[c]) * near[i] + summed[i][:, :HEAD_SIZE]) * inv_norm
            scaled[i], delta[i] = finish(rows, lanes[c], go_ref, out, inv_norm, near[i], o_ref, go_near_ref, delta_ref)

        def stage_dprobs(i):
            dprobs[i] = dot(scaled[i], v_t, ((1,), (0,)))

        def stage_dscores(i):
            dscores[i] = weights[i] * (dprobs[i] - delta[i]).astype(jnp.bfloat16)

        def stage_grads(i):
            row, c = chunks[i]
            store_heads(dq_ref, block_rows(row), lanes[c], dot(dscores[i], k, ((1,), (0,))))
            add_to(total, 1, dot(scaled[i], weights[i], ((0,), (0,))))
            add_to(total, 0, dot(q[i], dscores[i], ((0,), (0,))))

        skewed(
            len(chunks),
            [stage_scores, stage_weights, both(stage_summed, stage_out), both(stage_dprobs, stage_dscores), stage_grads],
        )
        dfar_ref[0] = (total[0] * INV_ROOT).astype(jnp.bfloat16).T
        dfar_ref[1] = total[1].astype(jnp.bfloat16).T


def body(ctx_size, query_states, key_states, value_state_rows, grad_out, vis_blocks, vis_count, vis_len):
    tokens, q_width = query_states.shape
    kv_width = key_states.shape[1]
    heads = kv_width // HEAD_SIZE
    per_shard = tokens // BLOCK
    vis = vis_blocks.shape[1]
    far = CAP * (ctx_size - 1)
    smem = pl.BlockSpec(memory_space=pltpu.SMEM)
    vmem = pl.BlockSpec(memory_space=pltpu.VMEM)
    hbm = pl.BlockSpec(memory_space=pltpu.HBM)
    bf16 = jnp.bfloat16
    pin = lambda array: pltpu.with_memory_space_constraint(array, pltpu.HBM)
    pair = ctx_size == 2
    sent_type = jax.ShapeDtypeStruct((2, ctx_size - 1, CAP * BLOCK, kv_width), bf16)
    busy = pl.CostEstimate(flops=10**10, bytes_accessed=2**20, transcendentals=0)
    small = pltpu.CompilerParams(vmem_limit_bytes=SMALL_VMEM)
    if pair:
        sent = pl.pallas_call(
            functools.partial(pack_pair_kernel, per_shard, vis),
            out_shape=[jax.ShapeDtypeStruct((2, 1, CAP * BLOCK, HEAD_SIZE), bf16)] * heads,
            in_specs=[smem, smem, hbm, hbm],
            out_specs=[vmem] * heads,
            scratch_shapes=[pltpu.VMEM((2, CAP * BLOCK, kv_width), bf16), pltpu.SemaphoreType.DMA((CAP, 2))],
            compiler_params=small,
            cost_estimate=busy,
            name="pack",
        )(pin(vis_blocks), pin(vis_count), pin(key_states), pin(value_state_rows))
    else:
        sent, plan = pl.pallas_call(
            functools.partial(pack_kernel, ctx_size, per_shard, vis),
            out_shape=[sent_type, jax.ShapeDtypeStruct((plan_size(ctx_size, per_shard, vis),), jnp.int32)],
            in_specs=[smem, smem, smem, hbm, hbm],
            out_specs=[vmem, smem],
            scratch_shapes=[
                pltpu.SMEM((ctx_size,), jnp.int32),
                pltpu.SemaphoreType.DMA((ctx_size - 1, per_shard, 2)),
            ],
            compiler_params=small,
            cost_estimate=busy,
            name="pack",
        )(pin(vis_blocks), pin(vis_count), pin(vis_len), pin(key_states), pin(value_state_rows))

    def move(array, back):
        parts = []
        for shift in range(1, ctx_size):
            pairs = [(i, i + shift) for i in range(ctx_size - shift)]
            if back:
                pairs = [(b, a) for a, b in pairs]
            parts.append(lax.ppermute(array[:, shift - 1 : shift], "ctx", pairs))
        return parts[0] if len(parts) == 1 else jnp.concatenate(parts, axis=1)

    if pair:
        got = [move(array, False).reshape(2, far * BLOCK, HEAD_SIZE) for array in reversed(sent)][::-1]
    else:
        got = move(sent, False).reshape(2, far * BLOCK, kv_width)
    q_type = jax.ShapeDtypeStruct(query_states.shape, bf16)
    part_type = jax.ShapeDtypeStruct(query_states.shape, jnp.float32)
    kv_type = jax.ShapeDtypeStruct(key_states.shape, bf16)
    weights_type = jax.ShapeDtypeStruct((per_shard, q_width // HEAD_SIZE * BLOCK, per_shard * BLOCK), bf16)
    flipped = lambda n, kind: pltpu.VMEM((heads, n, HEAD_SIZE, BLOCK), kind)
    large = pltpu.CompilerParams(vmem_limit_bytes=LARGE_VMEM + far // 4 * 2**20)
    flops = 2 * tokens * tokens * q_width
    cost = lambda n: pl.CostEstimate(flops=n * flops, bytes_accessed=8 * 2**20, transcendentals=0)
    lists = (pin(vis_blocks), pin(vis_count), pin(vis_len))
    part, top, norm, weights = pl.pallas_call(
        functools.partial(forward_kernel, ctx_size, per_shard, vis),
        out_shape=[part_type] * 3 + [weights_type],
        in_specs=[smem] * 3 + [vmem] * 3,
        out_specs=[vmem] * 4,
        compiler_params=large,
        cost_estimate=pl.CostEstimate(flops=2**20, bytes_accessed=2**20, transcendentals=0),
        name="forward_local",
    )(*lists, query_states, key_states, value_state_rows)
    far_types = [q_type, part_type, part_type, q_type]
    if pair:
        attention, dq_far, delta, go_near = None, part, top, None
        dfar = []
        for g in range(heads):
            before = [] if g == 0 else [attention, go_near]
            attention, dq_far, delta, go_near, array = pl.pallas_call(
                functools.partial(far_pair_kernel, per_shard, vis, heads, g),
                out_shape=far_types + [jax.ShapeDtypeStruct(got[g].shape, bf16)],
                in_specs=[smem] * 3 + [vmem] * (6 + len(before)),
                out_specs=[vmem] * 5,
                input_output_aliases={5: 1, 6: 2} | ({9: 0, 10: 3} if before else {}),
                compiler_params=large,
                cost_estimate=cost(3),
                name="far",
            )(*lists, query_states, grad_out, dq_far, delta, norm, got[g], *before)
            dfar.append(array)
    else:
        attention, dq_far, delta, go_near, dfar = pl.pallas_call(
            functools.partial(far_kernel, ctx_size, per_shard, vis),
            out_shape=far_types + [jax.ShapeDtypeStruct(got.shape, bf16)],
            grid_spec=pltpu.PrefetchScalarGridSpec(
                num_scalar_prefetch=1,
                grid=(per_shard,),
                in_specs=[vmem] * 6,
                out_specs=[vmem] * 5,
                scratch_shapes=[flipped(far, bf16)] * 2 + [flipped(far, jnp.float32)] * 2,
            ),
            input_output_aliases={3: 1, 4: 2},
            compiler_params=large,
            cost_estimate=cost(6),
            name="far",
        )(plan, query_states, grad_out, part, top, norm, got)
    if pair:
        returned = [move(array.reshape(2, 1, CAP * BLOCK, HEAD_SIZE), True) for array in dfar]
    else:
        returned = [move(dfar.reshape(sent.shape), True)]
    earlier = returned[:-1]
    own, attention, grad_query, dk, dv = pl.pallas_call(
        functools.partial(backward_kernel, ctx_size, per_shard, vis),
        out_shape=[jax.ShapeDtypeStruct((2, tokens, kv_width), bf16), q_type, q_type, kv_type, kv_type],
        in_specs=[vmem] * (8 + len(earlier)),
        out_specs=[vmem] + [hbm] * 4,
        scratch_shapes=[pltpu.VMEM((heads, HEAD_SIZE, tokens), jnp.float32)] * 2
        + [pltpu.VMEM(query_states.shape, bf16), pltpu.SemaphoreType.DMA((3 + per_shard,))],
        compiler_params=large,
        cost_estimate=cost(5),
        name="backward_local",
    )(query_states, go_near, dq_far, delta, weights, key_states, value_state_rows, attention, *earlier)
    add, lists = (add_pair_kernel, lists[:2]) if pair else (functools.partial(add_kernel, ctx_size), (plan,))
    grad_key, grad_value = pl.pallas_call(
        functools.partial(add, per_shard, vis),
        out_shape=[kv_type, kv_type],
        in_specs=[smem] * len(lists) + [vmem] * (1 + len(returned)) + [hbm, hbm],
        out_specs=[hbm, hbm],
        scratch_shapes=[
            pltpu.VMEM((2, tokens, kv_width), bf16),
            pltpu.SemaphoreType.DMA((2, per_shard)),
        ],
        input_output_aliases={len(lists) + len(returned) + 1: 0, len(lists) + len(returned) + 2: 1},
        compiler_params=small,
        name="add",
    )(*lists, own, *returned, dk, dv)
    return attention, grad_query, grad_key, grad_value


def solution(mesh):
    rows = P(("dp", "ctx"), "head")
    return jax.shard_map(
        functools.partial(body, mesh.shape["ctx"]),
        mesh=mesh,
        in_specs=(rows, rows, rows, rows, P("dp", None), P("dp"), P("dp", None)),
        out_specs=(rows, rows, rows, rows),
        check_vma=False,
    )
```

time: 252 us -> 31.2 us (0.12)
  local copies, waits for them, and re-layouts: 110 us -> 0.02 us
  matrix products: 53 us -> 0 us
  waiting for transfers between devices: 42.2 us -> 2.75 us
  other arithmetic: 29.7 us -> 0 us
  Pallas kernels: 0 us -> 19.7 us
  between operations: 14.1 us -> 0.94 us
  starting transfers between devices: 0.08 us -> 7.41 us
    dot_general x25 -> x0, matrix products: 53 us -> none  [the longest x4 17.8 us: attend(): jnp.einsum('qgrd,vkgd->grqvk', output_gradients, value_portion, preferred...]
    dynamic_update_slice x20 -> x0, local copies, waits for them, and re-layouts: 45.6 us -> none  [body(): lax.map(one_block, (query_states.reshape(per_shard, MASK_BLOCK_SIZE, -1),...]
    dynamic_slice x34 -> x0, local copies, waits for them, and re-layouts: 33.9 us -> none  [the longest x32 33.1 us: body(): lax.map(one_block, (query_states.reshape(per_shard, MASK_BLOCK_SIZE, -1),...]
    all_gather x1 -> x0, waiting for transfers between devices: 21.7 us -> none  [body(): gathered = lax.all_gather(local_kv, 'ctx', axis=0, tiled=True)]
    reduce_scatter x1 -> x0, waiting for transfers between devices: 20.5 us -> none  [body(): lax.psum_scatter(dense_part.reshape(total_blocks * MASK_BLOCK_SIZE, kv_to...]
    pallas_call x0 -> x6, Pallas kernels: none -> 19.7 us  [the longest x1 5.89 us: body(): pl.pallas_call(functools.partial(backward_kernel, ctx_size, per_shard, vi...]
    while x64 -> x0, local copies, waits for them, and re-layouts: 12.6 us -> none
    convert_element_type x4 -> x0, other arithmetic: 10.3 us -> none  [attend(): (soft_probs * (dprobs - row_delta) * inv_root).astype(jnp.bfloat16)]
  transfers between devices with their start and end apart: 2 -> 4, of which waited for: 2 -> 2; matrix products, arithmetic and copies ran while one was open for 1% -> 0% of each run, Pallas kernels for 0% -> 51%
where the time goes in v1:
time: 31.2 us; the launch traced here: 30.8 us
  Pallas kernels  19.7 us (63%)
  starting transfers between devices  7.41 us (24%)
  waiting for transfers between devices  2.75 us (9%)
  between operations  0.94 us (3%)
    ppermute x4, starting transfers between devices, move(): parts.append(lax.ppermute(array[:, shift - 1:shift], 'ctx', pairs))  7.41 us
    pallas_call x1, Pallas kernels, body(): pl.pallas_call(functools.partial(backward_kernel, ctx_size, per_shard, vi...  5.89 us
    pallas_call x1, Pallas kernels, body(): pl.pallas_call(functools.partial(forward_kernel, ctx_size, per_shard, vis...  5.04 us
    pallas_call x2, Pallas kernels, body(): pl.pallas_call(functools.partial(far_pair_kernel, per_shard, vis, heads,...  4.65 us
    ppermute x4, waiting for transfers between devices, move(): parts.append(lax.ppermute(array[:, shift - 1:shift], 'ctx', pairs))  2.75 us
    pallas_call x1, Pallas kernels, body(): pl.pallas_call(functools.partial(pack_pair_kernel, per_shard, vis), out_s...  2.39 us
    pallas_call x1, Pallas kernels, body(): pl.pallas_call(functools.partial(add, per_shard, vis), out_shape=[kv_type...  1.7 us
  transfers between devices with their start and end apart: 4, of which 2 were waited for; matrix products, arithmetic and copies ran while one was open for 0% of the time, Pallas kernels for 51%

profile of v1, /device:TPU:0, one launch (start us, length us, event | category | flops | bytes accessed | tf_op | source)
XLA Modules:
  0.0 30.8 jit_solution(1612988499986270785)
XLA Ops:
  0.6 0.0 copy-start.3
  0.6 0.0 copy-start.2
  0.7 0.0 copy-start
  0.7 0.0 copy-start.1
  0.7 2.4 %pack.1 = (bf16[2,1,256,128]{3,2,1,0:T(8,128)(2,1)S(1)}, bf16[2,1,256,128]{3,2,1,0:T(8,128)(2,1)S(1)}) custom-call(s32[8,6]{1,0:T(8,128)} %blocks_ref.9, s32[8]{0:T(128)} %count_ref.9, bf16[512,256]{1,0:T(8,128)(2,1)} %k_ref.5, bf16[512,256]{1,0:T(8,128)(2,1)} %v_ref.5), custom_call_target="tpu_custom_call" | custom-call | flops 10000000000 | bytes 1048576 | tf_op jit(solution)/shard_map/pack/pallas_call | solution.py:681
  3.1 3.5 %collective-permute-start = (bf16[2,1,256,128]{3,2,0,1:T(8,128)(2,1)S(1)}, bf16[2,1,256,128]{3,2,0,1:T(8,128)(2,1)S(1)}, u32[]{:S(2)}, u32[]{:S(2)}) collective-permute-start(bf16[2,1,256,128]{3,2,0,1:T(8,128)(2,1)S(1)} %bitcast.11), channel_id=1, source_target_pairs={{0,16},{1,17},{2,18},{3,19},{4,20},{5,21},{6,22},{7,23},{8,24},{9,... | collective-permute-start | bytes 393224 | tf_op jit(solution)/shard_map/ppermute | solution.py:712
  6.6 1.3 %collective-permute-start.1 = (bf16[2,1,256,128]{3,2,0,1:T(8,128)(2,1)S(1)}, bf16[2,1,256,128]{3,2,0,1:T(8,128)(2,1)S(1)}, u32[]{:S(2)}, u32[]{:S(2)}) collective-permute-start(bf16[2,1,256,128]{3,2,0,1:T(8,128)(2,1)S(1)} %bitcast.8), channel_id=1, source_target_pairs={{0,16},{1,17},{2,18},{3,19},{4,20},{5,21},{6,22},{7,23},{8,24},{9,... | collective-permute-start | bytes 393224 | tf_op jit(solution)/shard_map/ppermute | solution.py:712
  7.9 0.0 copy-done.3
  7.9 0.0 copy-done.2
  7.9 0.0 copy-done
  7.9 5.0 %forward_local.1 = (f32[512,2048]{1,0:T(8,128)S(1)}, f32[512,2048]{1,0:T(8,128)S(1)}, f32[512,2048]{1,0:T(8,128)S(1)}, bf16[4,2048,512]{2,1,0:T(8,128)(2,1)S(1)}) custom-call(s32[8,6]{1,0:T(8,128)} %blocks_ref.9, s32[8]{0:T(128)} %count_ref.9, s32[8,6]{1,0:T(8,128)} %lens_ref.5, bf16[512,2048]{1,0:T(8,128)(2,1)S(1)} %copy-done, ...), custom_call_target="tpu_custom_call" | custom-call | flops 1048576 | bytes 1048576 | tf_op jit(solution)/shard_map/forward_local/pallas_call | solution.py:728
  13.0 0.0 collective-permute-done
  13.0 0.0 copy-done.1
  13.0 2.2 %far.2 = (bf16[512,2048]{1,0:T(8,128)(2,1)S(1)}, f32[512,2048]{1,0:T(8,128)S(1)}, f32[512,2048]{1,0:T(8,128)S(1)}, bf16[512,2048]{1,0:T(8,128)(2,1)S(1)}, bf16[2,256,128]{2,1,0:T(8,128)(2,1)S(1)}) custom-call(s32[8,6]{1,0:T(8,128)} %blocks_ref.9, s32[8]{0:T(128)} %count_ref.9, s32[8,6]{1,0:T(8,128)} %lens_ref.5, ...), custom_call_target="tpu_custom_call", output_to_operand_aliasing={{1}: (5, {}), {2}: (6, {})} | custom-call | flops 3221225472 | bytes 8388608 | tf_op jit(solution)/shard_map/far/pallas_call | solution.py:743
  15.3 1.3 %collective-permute-start.2 = (bf16[2,1,256,128]{3,2,1,0:T(8,128)(2,1)S(1)}, bf16[2,1,256,128]{3,2,1,0:T(8,128)(2,1)S(1)}, u32[]{:S(2)}, u32[]{:S(2)}) collective-permute-start(bf16[2,1,256,128]{3,2,1,0:T(8,128)(2,1)S(1)} %bitcast.9), channel_id=1, source_target_pairs={{16,0},{17,1},{18,2},{19,3},{20,4},{21,5},{22,6},{23,7},{24,8},{25... | collective-permute-start | bytes 393224 | tf_op jit(solution)/shard_map/ppermute | solution.py:712
  16.6 0.0 collective-permute-done.1
  16.6 2.4 %far.3 = (bf16[512,2048]{1,0:T(8,128)(2,1)S(1)}, f32[512,2048]{1,0:T(8,128)S(1)}, f32[512,2048]{1,0:T(8,128)S(1)}, bf16[512,2048]{1,0:T(8,128)(2,1)S(1)}, bf16[2,256,128]{2,1,0:T(8,128)(2,1)S(1)}) custom-call(s32[8,6]{1,0:T(8,128)} %blocks_ref.9, s32[8]{0:T(128)} %count_ref.9, ...), custom_call_target="tpu_custom_call", output_to_operand_aliasing={{1}: (5, {}), {2}: (6, {}), {0}: (9, {}), {3}: (10, {})} | custom-call | flops 3221225472 | bytes 8388608 | tf_op jit(solution)/shard_map/far/pallas_call | solution.py:743
  19.0 1.3 %collective-permute-start.3 = (bf16[2,1,256,128]{3,2,1,0:T(8,128)(2,1)S(1)}, bf16[2,1,256,128]{3,2,1,0:T(8,128)(2,1)S(1)}, u32[]{:S(2)}, u32[]{:S(2)}) collective-permute-start(bf16[2,1,256,128]{3,2,1,0:T(8,128)(2,1)S(1)} %bitcast.10), channel_id=1, source_target_pairs={{16,0},{17,1},{18,2},{19,3},{20,4},{21,5},{22,6},{23,7},{24,8},{25... | collective-permute-start | bytes 393224 | tf_op jit(solution)/shard_map/ppermute | solution.py:712
  20.3 2.0 %collective-permute-done.2.rest_0_ = bf16[2,1,256,128]{3,2,1,0:T(8,128)(2,1)S(1)} collective-permute-done((bf16[2,1,256,128]{3,2,1,0:T(8,128)(2,1)S(1)}, bf16[2,1,256,128]{3,2,1,0:T(8,128)(2,1)S(1)}, u32[]{:S(2)}, u32[]{:S(2)}) %collective-permute-start.2) | collective-permute-done | bytes 131104 | tf_op jit(solution)/shard_map/ppermute | solution.py:712
  22.3 5.9 %backward_local.1 = (bf16[2,512,256]{2,1,0:T(8,128)(2,1)S(1)}, bf16[512,2048]{1,0:T(8,128)(2,1)}, bf16[512,2048]{1,0:T(8,128)(2,1)}, bf16[512,256]{1,0:T(8,128)(2,1)}, bf16[512,256]{1,0:T(8,128)(2,1)}) custom-call(bf16[512,2048]{1,0:T(8,128)(2,1)S(1)} %copy-done, bf16[512,2048]{1,0:T(8,128)(2,1)S(1)} %get-tuple-element.36.go_ref, ...), custom_call_target="tpu_custom_call" | custom-call | flops 5368709120 | bytes 8388608 | tf_op jit(solution)/shard_map/backward_local/pallas_call | solution.py:775
  28.2 0.7 %collective-permute-done.3.rest_1_ = bf16[2,1,256,128]{3,2,1,0:T(8,128)(2,1)S(1)} collective-permute-done((bf16[2,1,256,128]{3,2,1,0:T(8,128)(2,1)S(1)}, bf16[2,1,256,128]{3,2,1,0:T(8,128)(2,1)S(1)}, u32[]{:S(2)}, u32[]{:S(2)}) %collective-permute-start.3) | collective-permute-done | bytes 131104 | tf_op jit(solution)/shard_map/ppermute | solution.py:712
  28.9 1.7 %add.1 = (bf16[512,256]{1,0:T(8,128)(2,1)}, bf16[512,256]{1,0:T(8,128)(2,1)}) custom-call(s32[8,6]{1,0:T(8,128)} %blocks_ref.9, s32[8]{0:T(128)} %count_ref.9, bf16[2,512,256]{2,1,0:T(8,128)(2,1)S(1)} %get-tuple-element.44.own_ref, bf16[2,1,256,128]{3,2,1,0:T(8,128)(2,1)S(1)} %collective-permute-done.2.rest_0_, ...), custom_call_target="tpu_custom_call", output_to_operand_aliasing={{0}: (5, {}), {1}: (6, {})} | custom-call | tf_op jit(solution)/shard_map/add/pallas_call | solution.py:787
Async XLA Ops:
  0.6 7.3 %copy-start.3 = (bf16[512,256]{1,0:T(8,128)(2,1)S(1)}, bf16[512,256]{1,0:T(8,128)(2,1)}, u32[]{:S(2)}) copy-start(bf16[512,256]{1,0:T(8,128)(2,1)} %v_ref.5) | copy-start | bytes 786436
  0.6 7.3 %copy-start.2 = (bf16[512,256]{1,0:T(8,128)(2,1)S(1)}, bf16[512,256]{1,0:T(8,128)(2,1)}, u32[]{:S(2)}) copy-start(bf16[512,256]{1,0:T(8,128)(2,1)} %k_ref.5) | copy-start | bytes 786436
  0.7 7.3 %copy-start = (bf16[512,2048]{1,0:T(8,128)(2,1)S(1)}, bf16[512,2048]{1,0:T(8,128)(2,1)}, u32[]{:S(2)}) copy-start(bf16[512,2048]{1,0:T(8,128)(2,1)} %q_ref.7) | copy-start | bytes 6291460
  0.7 12.3 %copy-start.1 = (bf16[512,2048]{1,0:T(8,128)(2,1)S(1)}, bf16[512,2048]{1,0:T(8,128)(2,1)}, u32[]{:S(2)}) copy-start(bf16[512,2048]{1,0:T(8,128)(2,1)} %go_ref.3) | copy-start | bytes 6291460
  3.1 9.9 %collective-permute-start = (bf16[2,1,256,128]{3,2,0,1:T(8,128)(2,1)S(1)}, bf16[2,1,256,128]{3,2,0,1:T(8,128)(2,1)S(1)}, u32[]{:S(2)}, u32[]{:S(2)}) collective-permute-start(bf16[2,1,256,128]{3,2,0,1:T(8,128)(2,1)S(1)} %bitcast.11), channel_id=1, source_target_pairs={{0,16},{1,17},{2,18},{3,19},{4,20},{5,21},{6,22},{7,23},{8,24},{9,... | collective-permute-start | bytes 393224 | tf_op jit(solution)/shard_map/ppermute | solution.py:712
  6.6 9.9 %collective-permute-start.1 = (bf16[2,1,256,128]{3,2,0,1:T(8,128)(2,1)S(1)}, bf16[2,1,256,128]{3,2,0,1:T(8,128)(2,1)S(1)}, u32[]{:S(2)}, u32[]{:S(2)}) collective-permute-start(bf16[2,1,256,128]{3,2,0,1:T(8,128)(2,1)S(1)} %bitcast.8), channel_id=1, source_target_pairs={{0,16},{1,17},{2,18},{3,19},{4,20},{5,21},{6,22},{7,23},{8,24},{9,... | collective-permute-start | bytes 393224 | tf_op jit(solution)/shard_map/ppermute | solution.py:712
  15.3 7.1 %collective-permute-start.2 = (bf16[2,1,256,128]{3,2,1,0:T(8,128)(2,1)S(1)}, bf16[2,1,256,128]{3,2,1,0:T(8,128)(2,1)S(1)}, u32[]{:S(2)}, u32[]{:S(2)}) collective-permute-start(bf16[2,1,256,128]{3,2,1,0:T(8,128)(2,1)S(1)} %bitcast.9), channel_id=1, source_target_pairs={{16,0},{17,1},{18,2},{19,3},{20,4},{21,5},{22,6},{23,7},{24,8},{25... | collective-permute-start | bytes 393224 | tf_op jit(solution)/shard_map/ppermute | solution.py:712
  19.0 10.0 %collective-permute-start.3 = (bf16[2,1,256,128]{3,2,1,0:T(8,128)(2,1)S(1)}, bf16[2,1,256,128]{3,2,1,0:T(8,128)(2,1)S(1)}, u32[]{:S(2)}, u32[]{:S(2)}) collective-permute-start(bf16[2,1,256,128]{3,2,1,0:T(8,128)(2,1)S(1)} %bitcast.10), channel_id=1, source_target_pairs={{16,0},{17,1},{18,2},{19,3},{20,4},{21,5},{22,6},{23,7},{24,8},{25... | collective-permute-start | bytes 393224 | tf_op jit(solution)/shard_map/ppermute | solution.py:712

commit v2 on v1

--- a/solution.py
+++ b/solution.py
@@ -15,8 +15,9 @@
 MASKED = -1e30
 INV_ROOT = 1.0 / math.sqrt(HEAD_SIZE)
 EXP2_SCALE = INV_ROOT * math.log2(math.e)
+SUM_LIMIT = 2.0**96
 SMALL_VMEM = 8 * 1024 * 1024
-LARGE_VMEM = 16 * 1024 * 1024
+LARGE_VMEM = 14 * 1024 * 1024
 
 
 def dot(a, b, contract):
@@ -192,6 +193,10 @@
     return [[pl.ds((CHUNK * c + i) * HEAD_SIZE, HEAD_SIZE) for i in range(CHUNK)] for c in range(parts)]
 
 
+def row_lanes(row):
+    return pl.ds(row * (row + 1) // 2 * BLOCK, (row + 1) * BLOCK)
+
+
 def chunk_rows(c):
     return pl.ds(c * CHUNK * BLOCK, CHUNK * BLOCK)
 
@@ -258,12 +263,19 @@
     return pl.ds(row * BLOCK, BLOCK)
 
 
+def chunk_lanes(c):
+    at = [pl.multiple_of((CHUNK * c + i) * HEAD_SIZE, HEAD_SIZE) for i in range(CHUNK)]
+    return [pl.ds(x, HEAD_SIZE) for x in at]
+
+
 def forward_kernel(
-    ctx_size, per_shard, vis, blocks_ref, count_ref, lens_ref, q_ref, k_ref, v_ref, part_ref, top_ref, norm_ref, p_ref
+    ctx_size, per_shard, vis, blocks_ref, count_ref, lens_ref, q_ref, k_ref, v_ref,
+    part_ref, top_ref, norm_ref, p_ref, shifted_ref,
 ):
     kv_heads = k_ref.shape[1] // HEAD_SIZE
     lanes = head_lanes(q_ref.shape[1])
     parts = len(lanes)
+    per_kv = parts // kv_heads
     lengths = near_lengths(ctx_size, per_shard, vis, blocks_ref, count_ref, lens_ref)
     biases = [hidden_bias(near_masks(1, of_row)) for of_row in lengths]
     query_at, lane_at = iotas(CHUNK)
@@ -272,21 +284,22 @@
     k_t = [k_ref[:, at].T for at in heads_at]
     k_bias = [[jnp.concatenate([x[:, : bias.shape[1]], bias], axis=0) for x in k_t] for bias in biases]
     v_one = [with_ones(v_ref[:, at]) for at in heads_at]
-    chunks = [(row, c, c * kv_heads // parts) for row in range(per_shard) for c in range(parts)]
+    chunks = [(row, c, c // per_kv) for row in range(per_shard) for c in range(parts)]
     scores, weights, summed = ([None] * len(chunks) for _ in range(3))
+    bounds = [None, None]
+
+    def score(row, at, g):
+        q = rows_of_heads(q_ref, block_rows(row), at)
+        return dot(jnp.concatenate([q, which], axis=1), k_bias[row][g], ((1,), (0,)))
 
     def stage_scores(i):
         row, c, g = chunks[i]
-        q = rows_of_heads(q_ref, block_rows(row), lanes[c])
-        scores[i] = dot(jnp.concatenate([q, which], axis=1), k_bias[row][g], ((1,), (0,)))
+        scores[i] = score(row, lanes[c], g)
 
     def stage_weights(i):
         row, c, g = chunks[i]
-        seen = scores[i]
-        top = jnp.ceil(jnp.max(seen, axis=1, keepdims=True) * EXP2_SCALE)
-        weights[i] = jnp.exp2(seen * EXP2_SCALE - top).astype(jnp.bfloat16)
-        p_ref[row, chunk_rows(c), pl.ds(0, (row + 1) * BLOCK)] = weights[i]
-        store_heads(top_ref, block_rows(row), lanes[c], jnp.broadcast_to(top, (CHUNK * BLOCK, HEAD_SIZE)))
+        weights[i] = jnp.exp2(scores[i] * EXP2_SCALE).astype(jnp.bfloat16)
+        p_ref[chunk_rows(c), row_lanes(row)] = weights[i]
 
     def stage_summed(i):
         row, c, g = chunks[i]
@@ -294,10 +307,35 @@
 
     def stage_out(i):
         row, c, g = chunks[i]
+        norm = summed[i][:, HEAD_SIZE:]
         store_heads(part_ref, block_rows(row), lanes[c], summed[i][:, :HEAD_SIZE])
-        store_heads(norm_ref, block_rows(row), lanes[c], summed[i][:, HEAD_SIZE:])
+        store_heads(norm_ref, block_rows(row), lanes[c], norm)
+        bounds[0] = norm if i == 0 else jnp.minimum(bounds[0], norm)
+        bounds[1] = norm if i == 0 else jnp.maximum(bounds[1], norm)
 
     skewed(len(chunks), [stage_scores, stage_weights, stage_summed, stage_out])
+    good = (jnp.min(bounds[0]) > 1.0 / SUM_LIMIT) & (jnp.max(bounds[1]) < SUM_LIMIT)
+    shifted_ref[0] = jnp.where(good, 0, 1).astype(jnp.int32)
+
+    @pl.when(jnp.logical_not(good))
+    def _():
+        for row in range(per_shard):
+            for g in range(kv_heads):
+
+                def step(c, carry):
+                    at = chunk_lanes(c)
+                    seen = score(row, at, g)
+                    top = jnp.ceil(jnp.max(seen, axis=1, keepdims=True) * EXP2_SCALE)
+                    low = jnp.exp2(seen * EXP2_SCALE - top).astype(jnp.bfloat16)
+                    rows = pl.ds(pl.multiple_of(c * CHUNK * BLOCK, CHUNK * BLOCK), CHUNK * BLOCK)
+                    p_ref[rows, row_lanes(row)] = low
+                    out = dot(low, v_one[g][: (row + 1) * BLOCK], ((1,), (0,)))
+                    store_heads(top_ref, block_rows(row), at, jnp.broadcast_to(top, (CHUNK * BLOCK, HEAD_SIZE)))
+                    store_heads(part_ref, block_rows(row), at, out[:, :HEAD_SIZE])
+                    store_heads(norm_ref, block_rows(row), at, out[:, HEAD_SIZE:])
+                    return carry
+
+                lax.fori_loop(g * per_kv, (g + 1) * per_kv, step, 0)
 
 
 def backward_kernel(
@@ -324,7 +362,7 @@
     def stage_dscores(i):
         row, c, g = chunks[i]
         delta = repeat(rows_of_heads(delta_ref, block_rows(row), lanes[c]), row + 1)
-        weights[i] = p_ref[row, chunk_rows(c), pl.ds(0, (row + 1) * BLOCK)]
+        weights[i] = p_ref[chunk_rows(c), row_lanes(row)]
         dscores[i] = weights[i] * (dprobs[i] - delta).astype(jnp.bfloat16)
 
     def stage_grads(i):
@@ -363,6 +401,10 @@
         copy.wait()
 
 
+def known_top(shifted_ref, top_ref, rows, lanes):
+    return jnp.where(shifted_ref[0] == 1, rows_of_heads(top_ref, rows, lanes), 0.0)
+
+
 def finish(rows, lanes, go_ref, out, inv_norm, near, o_ref, go_near_ref, delta_ref):
     store_heads(o_ref, rows, lanes, out.astype(jnp.bfloat16))
     scaled = (rows_of_heads(go_ref, rows, lanes).astype(jnp.float32) * inv_norm).astype(jnp.bfloat16)
@@ -389,7 +431,7 @@
 
 
 def with_far(
-    slots, kv_heads, rows, q_ref, go_ref, part_ref, top_ref, norm_ref, far_ref, o_ref, dq_ref, go_near_ref, delta_ref,
+    slots, kv_heads, rows, shifted_ref, q_ref, go_ref, part_ref, top_ref, norm_ref, far_ref, o_ref, dq_ref, go_near_ref, delta_ref,
     kt_t, vt_t, acc_k, acc_v, pos, lens,
 ):
     lanes = head_lanes(q_ref.shape[1])
@@ -409,7 +451,7 @@
 
     def stage_weights(c):
         seen = hide(masks, scores[c])
-        top_near = rows_of_heads(top_ref, rows, lanes[c])
+        top_near = known_top(shifted_ref, top_ref, rows, lanes[c])
         top[c] = jnp.maximum(jnp.ceil(jnp.max(seen, axis=1, keepdims=True) * EXP2_SCALE), top_near)
         near[c] = jnp.exp2(top_near - top[c])
         weights[c] = jnp.exp2(seen * EXP2_SCALE - repeat(top[c], slots)).astype(jnp.bfloat16)
@@ -472,7 +514,7 @@
 
 
 def far_kernel(
-    ctx_size, per_shard, vis, plan_ref, q_ref, go_ref, part_ref, top_ref, norm_ref, far_ref,
+    ctx_size, per_shard, vis, plan_ref, shifted_ref, q_ref, go_ref, part_ref, top_ref, norm_ref, far_ref,
     o_ref, dq_ref, delta_ref, go_near_ref, dfar_ref, kt_t, vt_t, acc_k, acc_v,
 ):
     row, rows = step_rows()
@@ -494,7 +536,7 @@
 
     def run(slots, pos, lens):
         with_far(
-            slots, kv_heads, rows, q_ref, go_ref, part_ref, top_ref, norm_ref, far_ref, o_ref, dq_ref, go_near_ref, delta_ref,
+            slots, kv_heads, rows, shifted_ref, q_ref, go_ref, part_ref, top_ref, norm_ref, far_ref, o_ref, dq_ref, go_near_ref, delta_ref,
             kt_t, vt_t, acc_k, acc_v, pos, lens,
         )
 
@@ -578,10 +620,10 @@
 
 
 def far_pair_kernel(
-    per_shard, vis, kv_heads, g, blocks_ref, count_ref, lens_ref, q_ref, go_ref, part_ref, top_ref, norm_ref, far_ref,
-    *rest
+    per_shard, vis, kv_heads, g, blocks_ref, count_ref, lens_ref, shifted_ref, q_ref, go_ref, part_ref, top_ref, norm_ref,
+    far_ref, *rest
 ):
-    o_ref, dq_ref, delta_ref, go_near_ref, dfar_ref = rest[-5:]
+    o_ref, dq_ref, delta_ref, go_near_ref, dfar_ref, again_ref = rest[-6:]
     me = lax.axis_index("ctx")
     lanes = head_lanes(q_ref.shape[1])
     per_kv = len(lanes) // kv_heads
@@ -596,27 +638,28 @@
         dq_ref[:, all_lanes] = jnp.zeros((dq_ref.shape[0], all_lanes.size), dq_ref.dtype)
         dfar_ref[...] = jnp.zeros_like(dfar_ref)
 
-    @pl.when(some)
-    def _():
-        earlier = (me - 1) * per_shard
-        masks = []
-        for row in range(per_shard):
-            at = me * per_shard + row
-            count = count_ref[at]
-            lens = [jnp.int32(0), jnp.int32(0)]
-            for slot in range(1, vis):
-                block, visible = blocks_ref[at, slot], lens_ref[at, slot]
-                live = slot < count
-                lens[0] = lens[0] + jnp.where(live & (block == earlier + first), visible, 0)
-                lens[1] = lens[1] + jnp.where(live & (block == earlier + second) & (first != second), visible, 0)
-            masks.append(far_masks(CHUNK, lens))
-        k, v = far_ref[0], far_ref[1]
+    again_ref[0] = jnp.where(some, shifted_ref[0], 0)
+    earlier = (me - 1) * per_shard
+    masks = []
+    for row in range(per_shard):
+        at = me * per_shard + row
+        count = count_ref[at]
+        lens = [jnp.int32(0), jnp.int32(0)]
+        for slot in range(1, vis):
+            block, visible = blocks_ref[at, slot], lens_ref[at, slot]
+            live = slot < count
+            lens[0] = lens[0] + jnp.where(live & (block == earlier + first), visible, 0)
+            lens[1] = lens[1] + jnp.where(live & (block == earlier + second) & (first != second), visible, 0)
+        masks.append(far_masks(CHUNK, lens))
+    k, v = far_ref[0], far_ref[1]
+
+    @pl.when(some & (shifted_ref[0] == 0))
+    def _():
         k_t, v_t, v_one = k.T, v.T, with_ones(v)
         chunks = [(row, c) for row in range(per_shard) for c in range(per_kv)]
-        q, scores, top, near, weights, summed, scaled, delta, dprobs, dscores = (
-            [None] * len(chunks) for _ in range(10)
-        )
+        q, scores, weights, summed, scaled, delta, dprobs, dscores = ([None] * len(chunks) for _ in range(8))
         total = {}
+        bound = [None]
 
         def stage_scores(i):
             row, c = chunks[i]
@@ -624,12 +667,7 @@
             scores[i] = dot(q[i], k_t, ((1,), (0,)))
 
         def stage_weights(i):
-            row, c = chunks[i]
-            seen = hide(masks[row], scores[i])
-            top_near = rows_of_heads(top_ref, block_rows(row), lanes[c])
-            top[i] = jnp.maximum(jnp.ceil(jnp.max(seen, axis=1, keepdims=True) * EXP2_SCALE), top_near)
-            near[i] = jnp.exp2(top_near - top[i])
-            weights[i] = jnp.exp2(seen * EXP2_SCALE - repeat(top[i], CAP)).astype(jnp.bfloat16)
+            weights[i] = jnp.exp2(hide(masks[chunks[i][0]], scores[i]) * EXP2_SCALE).astype(jnp.bfloat16)
 
         def stage_summed(i):
             summed[i] = dot(weights[i], v_one, ((1,), (0,)))
@@ -637,9 +675,11 @@
         def stage_out(i):
             row, c = chunks[i]
             rows = block_rows(row)
-            inv_norm = 1.0 / (near[i] * rows_of_heads(norm_ref, rows, lanes[c]) + summed[i][:, HEAD_SIZE:])
-            out = (rows_of_heads(part_ref, rows, lanes[c]) * near[i] + summed[i][:, :HEAD_SIZE]) * inv_norm
-            scaled[i], delta[i] = finish(rows, lanes[c], go_ref, out, inv_norm, near[i], o_ref, go_near_ref, delta_ref)
+            norm = rows_of_heads(norm_ref, rows, lanes[c]) + summed[i][:, HEAD_SIZE:]
+            bound[0] = norm if i == 0 else jnp.maximum(bound[0], norm)
+            inv_norm = 1.0 / norm
+            out = (rows_of_heads(part_ref, rows, lanes[c]) + summed[i][:, :HEAD_SIZE]) * inv_norm
+            scaled[i], delta[i] = finish(rows, lanes[c], go_ref, out, inv_norm, None, o_ref, go_near_ref, delta_ref)
 
         def stage_dprobs(i):
             dprobs[i] = dot(scaled[i], v_t, ((1,), (0,)))
@@ -657,6 +697,36 @@
             len(chunks),
             [stage_scores, stage_weights, both(stage_summed, stage_out), both(stage_dprobs, stage_dscores), stage_grads],
         )
+        dfar_ref[0] = (total[0] * INV_ROOT).astype(jnp.bfloat16).T
+        dfar_ref[1] = total[1].astype(jnp.bfloat16).T
+        again_ref[0] = jnp.where(jnp.max(bound[0]) < SUM_LIMIT, 0, 1).astype(jnp.int32)
+
+    @pl.when(again_ref[0] == 1)
+    def _():
+        k_t, v_t, v_one = k.T, v.T, with_ones(v)
+        total = (jnp.zeros((HEAD_SIZE, CAP * BLOCK), jnp.float32),) * 2
+        for row in range(per_shard):
+            rows = block_rows(row)
+
+            def step(c, total):
+                at = chunk_lanes(c)
+                q = rows_of_heads(q_ref, rows, at)
+                seen = hide(masks[row], dot(q, k_t, ((1,), (0,))))
+                top_near = known_top(shifted_ref, top_ref, rows, at)
+                top = jnp.maximum(jnp.ceil(jnp.max(seen, axis=1, keepdims=True) * EXP2_SCALE), top_near)
+                near = jnp.exp2(top_near - top)
+                weights = jnp.exp2(seen * EXP2_SCALE - repeat(top, CAP)).astype(jnp.bfloat16)
+                summed = dot(weights, v_one, ((1,), (0,)))
+                inv_norm = 1.0 / (near * rows_of_heads(norm_ref, rows, at) + summed[:, HEAD_SIZE:])
+                out = (rows_of_heads(part_ref, rows, at) * near + summed[:, :HEAD_SIZE]) * inv_norm
+                scaled, delta = finish(rows, at, go_ref, out, inv_norm, near, o_ref, go_near_ref, delta_ref)
+                dprobs = dot(scaled, v_t, ((1,), (0,)))
+                dscores = weights * (dprobs - delta).astype(jnp.bfloat16)
+                store_heads(dq_ref, rows, at, dot(dscores, k, ((1,), (0,))))
+                grads = dot(q, dscores, ((0,), (0,))), dot(scaled, weights, ((0,), (0,)))
+                return total[0] + grads[0], total[1] + grads[1]
+
+            total = lax.fori_loop(g * per_kv, (g + 1) * per_kv, step, total)
         dfar_ref[0] = (total[0] * INV_ROOT).astype(jnp.bfloat16).T
         dfar_ref[1] = total[1].astype(jnp.bfloat16).T
 
@@ -719,54 +789,53 @@
     q_type = jax.ShapeDtypeStruct(query_states.shape, bf16)
     part_type = jax.ShapeDtypeStruct(query_states.shape, jnp.float32)
     kv_type = jax.ShapeDtypeStruct(key_states.shape, bf16)
-    weights_type = jax.ShapeDtypeStruct((per_shard, q_width // HEAD_SIZE * BLOCK, per_shard * BLOCK), bf16)
+    weights_type = jax.ShapeDtypeStruct((q_width, per_shard * (per_shard + 1) // 2 * BLOCK), bf16)
     flipped = lambda n, kind: pltpu.VMEM((heads, n, HEAD_SIZE, BLOCK), kind)
     large = pltpu.CompilerParams(vmem_limit_bytes=LARGE_VMEM + far // 4 * 2**20)
     flops = 2 * tokens * tokens * q_width
     cost = lambda n: pl.CostEstimate(flops=n * flops, bytes_accessed=8 * 2**20, transcendentals=0)
     lists = (pin(vis_blocks), pin(vis_count), pin(vis_len))
-    part, top, norm, weights = pl.pallas_call(
+    part, top, norm, weights, shifted = pl.pallas_call(
         functools.partial(forward_kernel, ctx_size, per_shard, vis),
-        out_shape=[part_type] * 3 + [weights_type],
+        out_shape=[part_type] * 3 + [weights_type, jax.ShapeDtypeStruct((1,), jnp.int32)],
         in_specs=[smem] * 3 + [vmem] * 3,
-        out_specs=[vmem] * 4,
+        out_specs=[vmem] * 4 + [smem],
         compiler_params=large,
         cost_estimate=pl.CostEstimate(flops=2**20, bytes_accessed=2**20, transcendentals=0),
         name="forward_local",
     )(*lists, query_states, key_states, value_state_rows)
     far_types = [q_type, part_type, part_type, q_type]
     if pair:
-        attention, dq_far, delta, go_near = None, part, top, None
-        dfar = []
+        dfar, before = [], []
         for g in range(heads):
-            before = [] if g == 0 else [attention, go_near]
-            attention, dq_far, delta, go_near, array = pl.pallas_call(
+            *before, array = pl.pallas_call(
                 functools.partial(far_pair_kernel, per_shard, vis, heads, g),
                 out_shape=far_types + [jax.ShapeDtypeStruct(got[g].shape, bf16)],
-                in_specs=[smem] * 3 + [vmem] * (6 + len(before)),
+                in_specs=[smem] * 4 + [vmem] * (6 + len(before)),
                 out_specs=[vmem] * 5,
-                input_output_aliases={5: 1, 6: 2} | ({9: 0, 10: 3} if before else {}),
+                scratch_shapes=[pltpu.SMEM((1,), jnp.int32)],
+                input_output_aliases={10 + i: i for i in range(len(before))},
                 compiler_params=large,
                 cost_estimate=cost(3),
                 name="far",
-            )(*lists, query_states, grad_out, dq_far, delta, norm, got[g], *before)
+            )(*lists, shifted, query_states, grad_out, part, top, norm, got[g], *before)
             dfar.append(array)
+        attention, dq_far, delta, go_near = before
     else:
         attention, dq_far, delta, go_near, dfar = pl.pallas_call(
             functools.partial(far_kernel, ctx_size, per_shard, vis),
             out_shape=far_types + [jax.ShapeDtypeStruct(got.shape, bf16)],
             grid_spec=pltpu.PrefetchScalarGridSpec(
-                num_scalar_prefetch=1,
+                num_scalar_prefetch=2,
                 grid=(per_shard,),
                 in_specs=[vmem] * 6,
                 out_specs=[vmem] * 5,
                 scratch_shapes=[flipped(far, bf16)] * 2 + [flipped(far, jnp.float32)] * 2,
             ),
-            input_output_aliases={3: 1, 4: 2},
             compiler_params=large,
             cost_estimate=cost(6),
             name="far",
-        )(plan, query_states, grad_out, part, top, norm, got)
+        )(plan, shifted, query_states, grad_out, part, top, norm, got)
     if pair:
         returned = [move(array.reshape(2, 1, CAP * BLOCK, HEAD_SIZE), True) for array in dfar]
     else:

time: 31.2 us -> 62.6 us (2.01)
  Pallas kernels: 19.7 us -> 35.4 us
  waiting for transfers between devices: 2.75 us -> 18.2 us
    ppermute x4, waiting for transfers between devices: 2.75 us -> 18.2 us  [move(): parts.append(lax.ppermute(array[:, shift - 1:shift], 'ctx', pairs))]
    pallas_call x1, Pallas kernels: 5.04 us -> 19.9 us  [body(): pl.pallas_call(functools.partial(forward_kernel, ctx_size, per_shard, vis...]
    pallas_call x2, Pallas kernels: 4.65 us -> 5.41 us  [body(): pl.pallas_call(functools.partial(far_pair_kernel, per_shard, vis, heads,...]
  transfers between devices with their start and end apart: 4 -> 4, of which waited for: 2 -> 2; matrix products, arithmetic and copies ran while one was open for 0% -> 0% of each run, Pallas kernels for 51% -> 50%
where the time goes in v2:
time: 62.6 us; the launch traced here: 62.3 us
  Pallas kernels  35.4 us (57%)
  waiting for transfers between devices  18.2 us (29%)
  starting transfers between devices  7.63 us (12%)
  between operations  0.96 us (2%)
    pallas_call x1, Pallas kernels, body(): pl.pallas_call(functools.partial(forward_kernel, ctx_size, per_shard, vis...  19.9 us
    ppermute x4, waiting for transfers between devices, move(): parts.append(lax.ppermute(array[:, shift - 1:shift], 'ctx', pairs))  18.2 us
    ppermute x4, starting transfers between devices, move(): parts.append(lax.ppermute(array[:, shift - 1:shift], 'ctx', pairs))  7.63 us
    pallas_call x1, Pallas kernels, body(): pl.pallas_call(functools.partial(backward_kernel, ctx_size, per_shard, vi...  6.04 us
    pallas_call x2, Pallas kernels, body(): pl.pallas_call(functools.partial(far_pair_kernel, per_shard, vis, heads,...  5.41 us
    pallas_call x1, Pallas kernels, body(): pl.pallas_call(functools.partial(pack_pair_kernel, per_shard, vis), out_s...  2.39 us
    pallas_call x1, Pallas kernels, body(): pl.pallas_call(functools.partial(add, per_shard, vis), out_shape=[kv_type...  1.7 us
  transfers between devices with their start and end apart: 4, of which 2 were waited for; matrix products, arithmetic and copies ran while one was open for 0% of the time, Pallas kernels for 50%

profile of v2, /device:TPU:0, one launch (start us, length us, event | category | flops | bytes accessed | tf_op | source)
XLA Modules:
  0.0 62.3 jit_solution(6996307705931370712)
XLA Ops:
  0.6 0.0 copy-start.3
  0.6 0.0 copy-start.2
  0.7 0.0 copy-start
  0.7 0.0 copy-start.1
  0.7 2.4 %pack.1 = (bf16[2,1,256,128]{3,2,1,0:T(8,128)(2,1)S(1)}, bf16[2,1,256,128]{3,2,1,0:T(8,128)(2,1)S(1)}) custom-call(s32[8,6]{1,0:T(8,128)} %blocks_ref.9, s32[8]{0:T(128)} %count_ref.9, bf16[512,256]{1,0:T(8,128)(2,1)} %k_ref.5, bf16[512,256]{1,0:T(8,128)(2,1)} %v_ref.5), custom_call_target="tpu_custom_call" | custom-call | flops 10000000000 | bytes 1048576 | tf_op jit(solution)/shard_map/pack/pallas_call | solution.py:751
  3.1 3.5 %collective-permute-start.1 = (bf16[2,1,256,128]{3,2,0,1:T(8,128)(2,1)S(1)}, bf16[2,1,256,128]{3,2,0,1:T(8,128)(2,1)S(1)}, u32[]{:S(2)}, u32[]{:S(2)}) collective-permute-start(bf16[2,1,256,128]{3,2,0,1:T(8,128)(2,1)S(1)} %bitcast.11), channel_id=1, source_target_pairs={{0,16},{1,17},{2,18},{3,19},{4,20},{5,21},{6,22},{7,23},{8,24},{9,... | collective-permute-start | bytes 393224 | tf_op jit(solution)/shard_map/ppermute | solution.py:782
  6.6 1.3 %collective-permute-start = (bf16[2,1,256,128]{3,2,0,1:T(8,128)(2,1)S(1)}, bf16[2,1,256,128]{3,2,0,1:T(8,128)(2,1)S(1)}, u32[]{:S(2)}, u32[]{:S(2)}) collective-permute-start(bf16[2,1,256,128]{3,2,0,1:T(8,128)(2,1)S(1)} %bitcast.8), channel_id=1, source_target_pairs={{0,16},{1,17},{2,18},{3,19},{4,20},{5,21},{6,22},{7,23},{8,24},{9,... | collective-permute-start | bytes 393224 | tf_op jit(solution)/shard_map/ppermute | solution.py:782
  7.9 0.0 copy-done.3
  7.9 0.0 copy-done.2
  7.9 0.0 copy-done
  7.9 19.9 %forward_local.1 = (f32[512,2048]{1,0:T(8,128)S(1)}, f32[512,2048]{1,0:T(8,128)S(1)}, f32[512,2048]{1,0:T(8,128)S(1)}, bf16[2048,1280]{1,0:T(8,128)(2,1)S(1)}, s32[1]{0:T(128)}) custom-call(s32[8,6]{1,0:T(8,128)} %blocks_ref.9, s32[8]{0:T(128)} %count_ref.9, s32[8,6]{1,0:T(8,128)} %lens_ref.5, bf16[512,2048]{1,0:T(8,128)(2,1)S(1)} %copy-done, ...), custom_call_target="tpu_custom_call" | custom-call | flops 1048576 | bytes 1048576 | tf_op jit(solution)/shard_map/forward_local/pallas_call | solution.py:798
  27.9 0.0 collective-permute-done.1
  27.9 0.0 copy-done.1
  27.9 2.8 %far.2 = (bf16[512,2048]{1,0:T(8,128)(2,1)S(1)}, f32[512,2048]{1,0:T(8,128)S(1)}, f32[512,2048]{1,0:T(8,128)S(1)}, bf16[512,2048]{1,0:T(8,128)(2,1)S(1)}, bf16[2,256,128]{2,1,0:T(8,128)(2,1)S(1)}) custom-call(s32[8,6]{1,0:T(8,128)} %blocks_ref.9, s32[8]{0:T(128)} %count_ref.9, s32[8,6]{1,0:T(8,128)} %lens_ref.5, s32[1]{0:T(128)} %get-tuple-element.28.shifted_ref, ...), custom_call_target="tpu_custom_call" | custom-call | flops 3221225472 | bytes 8388608 | tf_op jit(solution)/shard_map/far/pallas_call | solution.py:811
  30.7 1.3 %collective-permute-start.2 = (bf16[2,1,256,128]{3,2,1,0:T(8,128)(2,1)S(1)}, bf16[2,1,256,128]{3,2,1,0:T(8,128)(2,1)S(1)}, u32[]{:S(2)}, u32[]{:S(2)}) collective-permute-start(bf16[2,1,256,128]{3,2,1,0:T(8,128)(2,1)S(1)} %bitcast.10), channel_id=1, source_target_pairs={{16,0},{17,1},{18,2},{19,3},{20,4},{21,5},{22,6},{23,7},{24,8},{25... | collective-permute-start | bytes 393224 | tf_op jit(solution)/shard_map/ppermute | solution.py:782
  32.0 0.0 collective-permute-done
  32.0 2.6 %far.3 = (bf16[512,2048]{1,0:T(8,128)(2,1)S(1)}, f32[512,2048]{1,0:T(8,128)S(1)}, f32[512,2048]{1,0:T(8,128)S(1)}, bf16[512,2048]{1,0:T(8,128)(2,1)S(1)}, bf16[2,256,128]{2,1,0:T(8,128)(2,1)S(1)}) custom-call(s32[8,6]{1,0:T(8,128)} %blocks_ref.9, s32[8]{0:T(128)} %count_ref.9, ...), custom_call_target="tpu_custom_call", output_to_operand_aliasing={{0}: (10, {}), {1}: (11, {}), {2}: (12, {}), {3}: (13, {})} | custom-call | flops 3221225472 | bytes 8388608 | tf_op jit(solution)/shard_map/far/pallas_call | solution.py:811
  34.6 1.5 %collective-permute-start.3 = (bf16[2,1,256,128]{3,2,1,0:T(8,128)(2,1)S(1)}, bf16[2,1,256,128]{3,2,1,0:T(8,128)(2,1)S(1)}, u32[]{:S(2)}, u32[]{:S(2)}) collective-permute-start(bf16[2,1,256,128]{3,2,1,0:T(8,128)(2,1)S(1)} %bitcast.9), channel_id=1, source_target_pairs={{16,0},{17,1},{18,2},{19,3},{20,4},{21,5},{22,6},{23,7},{24,8},{25... | collective-permute-start | bytes 393224 | tf_op jit(solution)/shard_map/ppermute | solution.py:782
  36.1 9.5 %collective-permute-done.2.rest_0_ = bf16[2,1,256,128]{3,2,1,0:T(8,128)(2,1)S(1)} collective-permute-done((bf16[2,1,256,128]{3,2,1,0:T(8,128)(2,1)S(1)}, bf16[2,1,256,128]{3,2,1,0:T(8,128)(2,1)S(1)}, u32[]{:S(2)}, u32[]{:S(2)}) %collective-permute-start.2) | collective-permute-done | bytes 131104 | tf_op jit(solution)/shard_map/ppermute | solution.py:782
  45.6 6.0 %backward_local.1 = (bf16[2,512,256]{2,1,0:T(8,128)(2,1)S(1)}, bf16[512,2048]{1,0:T(8,128)(2,1)}, bf16[512,2048]{1,0:T(8,128)(2,1)}, bf16[512,256]{1,0:T(8,128)(2,1)}, bf16[512,256]{1,0:T(8,128)(2,1)}) custom-call(bf16[512,2048]{1,0:T(8,128)(2,1)S(1)} %copy-done, bf16[512,2048]{1,0:T(8,128)(2,1)S(1)} %get-tuple-element.38.go_ref, ...), custom_call_target="tpu_custom_call" | custom-call | flops 5368709120 | bytes 8388608 | tf_op jit(solution)/shard_map/backward_local/pallas_call | solution.py:844
  51.7 8.7 %collective-permute-done.3.rest_1_ = bf16[2,1,256,128]{3,2,1,0:T(8,128)(2,1)S(1)} collective-permute-done((bf16[2,1,256,128]{3,2,1,0:T(8,128)(2,1)S(1)}, bf16[2,1,256,128]{3,2,1,0:T(8,128)(2,1)S(1)}, u32[]{:S(2)}, u32[]{:S(2)}) %collective-permute-start.3) | collective-permute-done | bytes 131104 | tf_op jit(solution)/shard_map/ppermute | solution.py:782
  60.4 1.7 %add.1 = (bf16[512,256]{1,0:T(8,128)(2,1)}, bf16[512,256]{1,0:T(8,128)(2,1)}) custom-call(s32[8,6]{1,0:T(8,128)} %blocks_ref.9, s32[8]{0:T(128)} %count_ref.9, bf16[2,512,256]{2,1,0:T(8,128)(2,1)S(1)} %get-tuple-element.46.own_ref, bf16[2,1,256,128]{3,2,1,0:T(8,128)(2,1)S(1)} %collective-permute-done.2.rest_0_, ...), custom_call_target="tpu_custom_call", output_to_operand_aliasing={{0}: (5, {}), {1}: (6, {})} | custom-call | tf_op jit(solution)/shard_map/add/pallas_call | solution.py:856
Async XLA Ops:
  0.6 7.3 %copy-start.3 = (bf16[512,256]{1,0:T(8,128)(2,1)S(1)}, bf16[512,256]{1,0:T(8,128)(2,1)}, u32[]{:S(2)}) copy-start(bf16[512,256]{1,0:T(8,128)(2,1)} %v_ref.5) | copy-start | bytes 786436
  0.6 7.3 %copy-start.2 = (bf16[512,256]{1,0:T(8,128)(2,1)S(1)}, bf16[512,256]{1,0:T(8,128)(2,1)}, u32[]{:S(2)}) copy-start(bf16[512,256]{1,0:T(8,128)(2,1)} %k_ref.5) | copy-start | bytes 786436
  0.7 7.3 %copy-start = (bf16[512,2048]{1,0:T(8,128)(2,1)S(1)}, bf16[512,2048]{1,0:T(8,128)(2,1)}, u32[]{:S(2)}) copy-start(bf16[512,2048]{1,0:T(8,128)(2,1)} %q_ref.7) | copy-start | bytes 6291460
  0.7 27.2 %copy-start.1 = (bf16[512,2048]{1,0:T(8,128)(2,1)S(1)}, bf16[512,2048]{1,0:T(8,128)(2,1)}, u32[]{:S(2)}) copy-start(bf16[512,2048]{1,0:T(8,128)(2,1)} %go_ref.3) | copy-start | bytes 6291460
  3.1 24.8 %collective-permute-start.1 = (bf16[2,1,256,128]{3,2,0,1:T(8,128)(2,1)S(1)}, bf16[2,1,256,128]{3,2,0,1:T(8,128)(2,1)S(1)}, u32[]{:S(2)}, u32[]{:S(2)}) collective-permute-start(bf16[2,1,256,128]{3,2,0,1:T(8,128)(2,1)S(1)} %bitcast.11), channel_id=1, source_target_pairs={{0,16},{1,17},{2,18},{3,19},{4,20},{5,21},{6,22},{7,23},{8,24},{9,... | collective-permute-start | bytes 393224 | tf_op jit(solution)/shard_map/ppermute | solution.py:782
  6.6 25.3 %collective-permute-start = (bf16[2,1,256,128]{3,2,0,1:T(8,128)(2,1)S(1)}, bf16[2,1,256,128]{3,2,0,1:T(8,128)(2,1)S(1)}, u32[]{:S(2)}, u32[]{:S(2)}) collective-permute-start(bf16[2,1,256,128]{3,2,0,1:T(8,128)(2,1)S(1)} %bitcast.8), channel_id=1, source_target_pairs={{0,16},{1,17},{2,18},{3,19},{4,20},{5,21},{6,22},{7,23},{8,24},{9,... | collective-permute-start | bytes 393224 | tf_op jit(solution)/shard_map/ppermute | solution.py:782
  30.7 15.0 %collective-permute-start.2 = (bf16[2,1,256,128]{3,2,1,0:T(8,128)(2,1)S(1)}, bf16[2,1,256,128]{3,2,1,0:T(8,128)(2,1)S(1)}, u32[]{:S(2)}, u32[]{:S(2)}) collective-permute-start(bf16[2,1,256,128]{3,2,1,0:T(8,128)(2,1)S(1)} %bitcast.10), channel_id=1, source_target_pairs={{16,0},{17,1},{18,2},{19,3},{20,4},{21,5},{22,6},{23,7},{24,8},{25... | collective-permute-start | bytes 393224 | tf_op jit(solution)/shard_map/ppermute | solution.py:782
  34.6 25.8 %collective-permute-start.3 = (bf16[2,1,256,128]{3,2,1,0:T(8,128)(2,1)S(1)}, bf16[2,1,256,128]{3,2,1,0:T(8,128)(2,1)S(1)}, u32[]{:S(2)}, u32[]{:S(2)}) collective-permute-start(bf16[2,1,256,128]{3,2,1,0:T(8,128)(2,1)S(1)} %bitcast.9), channel_id=1, source_target_pairs={{16,0},{17,1},{18,2},{19,3},{20,4},{21,5},{22,6},{23,7},{24,8},{25... | collective-permute-start | bytes 393224 | tf_op jit(solution)/shard_map/ppermute | solution.py:782
